TPU v7x, 128 devices: a whole 4x4x4 slice. The times are simulated.
128 devices in a mesh: slab: 4 (over z_lo, core), dev: 32 (over y, z_hi, x).
Axes of the slice: x: 4, y: 4, z: 4 (z_hi: 2, z_lo: 2; z = z_hi * 2 + z_lo), core: 2. Of those that a mesh axis runs over, the one named last changes fastest.
Arguments:
- tilts: bfloat16 [32, 384, 3072], P('dev', 'slab'), may hold values from -6 to 6
- tilt_defocus: float32 [32], P('dev'), may hold values from 1 to 3
- defocus_table: float32 [8], replicated, may hold values from 0.2 to 1
- slab_pick: int32 [4], P('slab'), may hold values from 0 to 7
- interp_offset: int32 [32, 16], P(None, 'slab'), may hold values from -768 to 768
- interp_weights: bfloat16 [32, 16, 4], P(None, 'slab'), may hold values from -0.5 to 0.5
Outputs:
- volume: float32 [384, 16, 3072], P('dev', 'slab')
All inputs are finite; a program needn't handle non-finite values.
Results may differ from a plain program's by a relative error of at most 0.0029.
Values may be sent and summed in bfloat16 or wider, within the bound.
No kernel may reach another device: no remote copies, remote signals or barrier semaphores. Data moves between devices by JAX's collectives and lax.ppermute only.
A program may use at most 128 MiB of HBM per device.

v0:
```python
import math

import jax
import jax.numpy as jnp
from jax import lax
from jax.sharding import PartitionSpec as P

XP = 24
XQ = 128
YP = 3
YQ = 128
W = 3072
YB = 384
TAPS = 4


product_precision = lax.Precision.HIGH
two_pi = 2.0 * math.pi
chi_scale = 200.0
phase_shift = 0.1


def dft_table(length):
    counter = jnp.arange(length, dtype=jnp.int32)
    product = counter[:, None] * counter[None, :] % length
    angle = product.astype(jnp.float32) * (two_pi / length)
    return (jnp.cos(angle), jnp.sin(angle))


def twiddle_table(first, second):
    product = (
        jnp.arange(first, dtype=jnp.int32)[:, None] * jnp.arange(second, dtype=jnp.int32)[None, :]
    )
    angle = product.astype(jnp.float32) * (two_pi / (first * second))
    return (jnp.cos(angle), jnp.sin(angle))


def block_table(length, sign):
    table_cos, table_sin = dft_table(length)
    upper = jnp.stack([table_cos, -sign * table_sin])
    lower = jnp.stack([sign * table_sin, table_cos])
    return jnp.stack([upper, lower])


def section(form, paired, table):
    return jnp.einsum(form, paired, table, precision=product_precision)


def complex_twist(paired, twist_cos, twist_sin):
    real_part = paired[0]
    imag_part = paired[1]
    return jnp.stack(
        [
            real_part * twist_cos - imag_part * twist_sin,
            real_part * twist_sin + imag_part * twist_cos,
        ]
    )


def forward_rows(rows):
    count = rows.shape[0]
    shaped = rows.reshape(count, XP, XQ)
    cos_first, sin_first = dft_table(XP)
    first_table = jnp.stack([cos_first, -sin_first])
    twist_cos, twist_sin = twiddle_table(XP, XQ)
    paired = jnp.einsum("rpq,okp->orkq", shaped, first_table, precision=product_precision)
    paired = complex_twist(paired, twist_cos, -twist_sin)
    return section("irkq,oilq->orkl", paired, block_table(XQ, -1.0))


def inverse_rows(paired):
    count = paired.shape[1]
    cos_first, sin_first = dft_table(XP)
    last_table = jnp.stack([cos_first, -sin_first])
    twist_cos, twist_sin = twiddle_table(XP, XQ)
    paired = section("irkl,oiql->orkq", paired, block_table(XQ, 1.0))
    paired = complex_twist(paired, twist_cos, twist_sin)
    result = jnp.einsum("irkq,ipk->rpq", paired, last_table, precision=product_precision)
    return result.reshape(count, W)


def column_pass(paired, sign):
    twist_cos, twist_sin = twiddle_table(YP, YQ)
    twist_cos = twist_cos[:, :, None, None]
    twist_sin = twist_sin[:, :, None, None]
    if sign < 0:
        paired = paired.reshape(2, YP, YQ, XP, XQ)
        paired = section("iabkl,oica->ocbkl", paired, block_table(YP, -1.0))
        paired = complex_twist(paired, twist_cos, -twist_sin)
        return section("icbkl,oidb->ocdkl", paired, block_table(YQ, -1.0))
    paired = section("icdkl,oibd->ocbkl", paired, block_table(YQ, 1.0))
    paired = complex_twist(paired, twist_cos, twist_sin)
    paired = section("icbkl,oiac->oabkl", paired, block_table(YP, 1.0))
    return paired.reshape(2, YB, XP, XQ)


def squared_freq(index_grid, length):
    shifted = jnp.where(index_grid * 2 < length, index_grid, index_grid - length)
    scaled = shifted.astype(jnp.float32) / length
    return scaled * scaled


def response_grid(focus):
    row_index = (
        jnp.arange(YP, dtype=jnp.int32)[:, None] + YP * jnp.arange(YQ, dtype=jnp.int32)[None, :]
    )
    col_index = (
        jnp.arange(XP, dtype=jnp.int32)[:, None] + XP * jnp.arange(XQ, dtype=jnp.int32)[None, :]
    )
    radius = (
        squared_freq(row_index, YB)[:, :, None, None] + squared_freq(col_index, W)[None, None, :, :]
    )
    return -jnp.sin(chi_scale * focus * radius + phase_shift)


def body(tilts, tilt_defocus, defocus_table, slab_pick, interp_offset, interp_weights):
    entries = jnp.arange(defocus_table.shape[0], dtype=jnp.int32)
    group_defocus = jnp.sum(jnp.where(entries == slab_pick[0], defocus_table, 0.0))
    focus = tilt_defocus[0] + group_defocus
    whole = lax.all_gather(tilts, "slab", axis=1, tiled=True)
    paired = forward_rows(whole[0].astype(jnp.float32))
    paired = column_pass(paired, -1)
    response = response_grid(focus)
    paired = paired * response[None]
    paired = column_pass(paired, 1)
    restored = inverse_rows(paired) * (1.0 / (YB * W))
    filtered = restored.astype(jnp.bfloat16)
    moved = lax.all_to_all(filtered[None], "dev", split_axis=1, concat_axis=0, tiled=True)
    margin = W // 4 + TAPS
    padded = jnp.pad(moved, ((0, 0), (0, 0), (margin, margin)))
    row_count = moved.shape[1]

    def one_plane(pair):
        shift_col, weight_col = pair
        window = jax.vmap(
            lambda plane, start: lax.dynamic_slice_in_dim(plane, start, W + TAPS - 1, 1)
        )(padded, shift_col + margin)
        total = jnp.zeros((row_count, W), jnp.float32)
        for tap_index in range(TAPS):
            total = total + jnp.einsum(
                "tyx,t->yx",
                window[:, :, tap_index : tap_index + W],
                weight_col[:, tap_index],
                preferred_element_type=jnp.float32,
            )
        return total

    planes = lax.map(one_plane, (interp_offset.T, jnp.swapaxes(interp_weights, 0, 1)))
    return jnp.swapaxes(planes, 0, 1)


def solution(mesh):
    in_specs = (
        P("dev", "slab", None),
        P("dev"),
        P(),
        P("slab"),
        P(None, "slab"),
        P(None, "slab", None),
    )
    out_specs = P("dev", "slab", None)
    return jax.shard_map(body, mesh=mesh, in_specs=in_specs, out_specs=out_specs, check_vma=False)
```

profile of v0, /device:TPU:2, one launch (start us, length us, event | category | flops | bytes accessed | tf_op | source)
XLA Modules:
  0.0 734.2 jit_solution(9276456428264818261)
XLA Ops:
  15.1 17.1 %sine_negate_fusion = f32[3,128,24,128]{3,1,2,0:T(8,128)} fusion(f32[24,128]{1,0:T(8,128)S(1)} %fusion.79, f32[3,128]{1,0:T(4,128)S(1)} %fusion.97, f32[]{:T(128)S(6)} %mul_shard_map.3), kind=kLoop, calls=%fused_computation.60 | loop fusion | flops 4718592 | bytes 4732420 | tf_op jit(solution)/shard_map/neg | solution.py:113
  32.2 10.5 %all-gather.2.cloned.1.call-done = bf16[1,384,3072]{2,1,0:T(8,128)(2,1)} async-done(((bf16[1,96,3072]{2,1,0:T(8,128)(2,1)}), bf16[1,384,3072]{2,1,0:T(8,128)(2,1)}) %all-gather.2.cloned.1.call-update) | async-done | bytes 2359312 | tf_op jit(solution)/shard_map/all_gather | solution.py:120
  49.1 8.7 %fusion.48 = f32[2,384,24,128]{1,3,2,0:T(8,128)} fusion(f32[2,384,24,128]{3,2,1,0:T(8,128)S(1)} %pad_maximum_fusion.1, f32[1,2,128,128]{3,2,1,0:T(8,128)S(1)} %get-tuple-element.112, f32[1,2,128,128]{3,2,1,0:T(8,128)} %get-tuple-element.115), kind=kOutput, calls=%fused_computation.64 | convolution fusion | flops 3623944192 | bytes 19136512 | tf_op jit(solution)/shard_map/irkq,oilq->orkl/dot_general | solution.py:46
  57.8 9.6 %copy.53 = f32[2,384,24,128]{3,2,1,0:T(8,128)} copy(f32[2,384,24,128]{1,3,2,0:T(8,128)} %fusion.48) | data formatting | bytes 18874368 | tf_op jit(solution)/shard_map/irkq,oilq->orkl/transpose | solution.py:46
  67.4 29.0 %fusion.37 = f32[2,3,128,24,128]{4,1,3,2,0:T(4,128)} fusion(f32[2,3,128,24,128]{4,3,2,1,0:T(8,128)} %bitcast.214, f32[1,2,3,3]{3,2,1,0:T(4,128)S(1)} %copy.51, f32[1,2,3,3]{3,2,1,0:T(4,128)S(1)} %copy.50), kind=kOutput, calls=%fused_computation.53 | convolution fusion | flops 84934688 | bytes 18874512 | tf_op jit(solution)/shard_map/iabkl,oica->ocbkl/dot_general | solution.py:46
  96.4 7.3 multiply_subtract_fusion.1
  107.1 9.7 %fusion.30 = f32[2,128,3,24,128,1]{4,1,5,0,3,2:T(8,128)S(1)} fusion(f32[2,3,128,24,128,1]{4,1,3,2,0,5:T(4,128)S(1)} %maximum_bitcast_fusion, f32[1,2,128,128]{3,2,1,0:T(8,128)S(1)} %get-tuple-element.112, f32[1,2,128,128]{3,2,1,0:T(8,128)S(1)} %copy-done), kind=kOutput, calls=%fused_computation.42 | convolution fusion | flops 3623944192 | bytes 19136512 | tf_op jit(solution)/shard_map/icbkl,oidb->ocdkl/dot_general | solution.py:46
  116.8 7.3 fusion.51
  124.2 12.9 %copy.137 = f32[2,128,3,24,128]{4,2,3,1,0:T(4,128)S(1)} copy(f32[2,128,3,24,128]{4,1,3,2,0:T(8,128)} %fusion.51) | data formatting | bytes 18874368 | tf_op jit(solution)/shard_map/icdkl,oibd->ocbkl/dot_general | solution.py:46
  137.1 5.5 multiply_subtract_fusion
  142.7 21.0 %fusion.40 = f32[2,3,128,24,128]{4,1,3,2,0:T(4,128)} fusion(f32[1,2,3,3]{3,2,1,0:T(4,128)S(1)} %copy-done.6, f32[1,2,3,3]{3,2,1,0:T(4,128)S(1)} %copy.48, f32[1,3,128,24,128]{4,1,3,2,0:T(4,128)} %get-tuple-element.104, f32[1,3,128,24,128]{4,1,3,2,0:T(4,128)S(1)} %get-tuple-element.103), kind=kOutput, calls=%fused_computation.54 | convolution fusion | flops 87293984 | bytes 18874512 | tf_op jit(solution)/shard_map/icbkl,oiac->oabkl/dot_general | solution.py:46
  163.7 10.0 %copy.93 = f32[2,3,128,24,128]{4,2,1,0,3:T(8,128)S(1)} copy(f32[2,3,128,24,128]{4,1,3,2,0:T(4,128)} %fusion.40) | data formatting | bytes 18874368 | tf_op jit(solution)/shard_map/reshape | solution.py:94
  173.8 14.9 %fusion.45 = f32[2,384,24,128]{3,2,1,0:T(8,128)} fusion(f32[2,384,24,128,1]{3,1,0,2,4:T(8,128)S(1)} %bitcast.216, f32[1,2,128,128]{3,2,1,0:T(8,128)S(1)} %get-tuple-element.116, f32[1,2,128,128]{3,2,1,0:T(8,128)S(1)} %get-tuple-element.111), kind=kOutput, calls=%fused_computation.63 | convolution fusion | flops 3623944192 | bytes 19136512 | tf_op jit(solution)/shard_map/irkl,oiql->orkq/dot_general | solution.py:46
  197.1 6.4 convert_element_type.184
  204.0 14.2 %reduce.2 = bf16[384,3072]{1,0:T(8,128)(2,1)S(1)} reduce(bf16[384,1,3072]{2,1,0:T(2,128)(2,1)} %bitcast.218, bf16[]{:T(256)} %broadcast.591), dimensions={1}, to_apply=%bitcast.179.reduce_sub_computation | reduce | bytes 4718594
  220.9 10.1 %all-to-all-start = ((bf16[32,2,18432]{2,1,0:T(2,128)(2,1)}), bf16[32,2,18432]{2,1,0:T(2,128)(2,1)S(1)}, u32[]{:S(2)}, u32[]{:S(2)}) async-start(bf16[32,2,18432]{2,1,0:T(2,128)(2,1)} %reshape.457), calls=%async_computation | async-start | bytes 4718592 | tf_op jit(solution)/shard_map/all_to_all | solution.py:128
  231.0 35.0 %all-to-all-done = bf16[32,2,18432]{2,1,0:T(2,128)(2,1)S(1)} async-done(((bf16[32,2,18432]{2,1,0:T(2,128)(2,1)}), bf16[32,2,18432]{2,1,0:T(2,128)(2,1)S(1)}, u32[]{:S(2)}, u32[]{:S(2)}) %all-to-all-start) | async-done | bytes 2359328 | tf_op jit(solution)/shard_map/all_to_all | solution.py:128
  266.1 7.0 reshape.458
  273.1 16.4 %bitcast_reduce_fusion = bf16[384,3072]{1,0:T(8,128)(2,1)} fusion(bf16[384,1,3072]{2,1,0:T(2,128)(2,1)} %reshape.458), kind=kLoop, calls=%fused_computation.158 | loop fusion | bytes 4718592 | tf_op jit(solution)/shard_map/all_to_all | solution.py:128
  296.2 430.7 %while.15 = (s32[]{:T(128)}, f32[4,12,3072]{2,0,1:T(4,128)}, s32[4,32]{1,0:T(4,128)}, bf16[32,12,4616]{2,1,0:T(8,128)(2,1)}, bf16[4,32,4]{1,2,0:T(4,128)(2,1)}, /*index=5*/s32[]{:T(128)}, s32[]{:T(128)}, s32[]{:T(128)}) while((s32[]{:T(128)}, f32[4,12,3072]{2,0,1:T(4,128)}, s32[4,32]{1,0:T(4,128)}, bf16[32,12,4616]{2,1,0:T(8,128)(2,1)}, ...), condition=%wide.region_2.3_spmd, body=%wide.region_1.2_spmd.sunk | while | flops 9548004 | bytes 33554252 | solution.py:148
  296.9 93.7 %while.16 = (s32[]{:T(128)}, bf16[32,12,4616]{2,1,0:T(8,128)(2,1)}, s32[32,3]{0,1:T(4,128)S(1)}, bf16[32,12,3075]{2,1,0:T(8,128)(2,1)S(1)}, s32[]{:T(128)}) while((s32[]{:T(128)}, bf16[32,12,4616]{2,1,0:T(8,128)(2,1)}, s32[32,3]{0,1:T(4,128)S(1)}, bf16[32,12,3075]{2,1,0:T(8,128)(2,1)S(1)}, s32[]{:T(128)}) %tuple.65), condition=%wide.while_cond, body=%wide.while_body.sunk | while | flops 2 | bytes 176317 | solution.py:136
  404.6 93.7 %while.16 = (s32[]{:T(128)}, bf16[32,12,4616]{2,1,0:T(8,128)(2,1)}, s32[32,3]{0,1:T(4,128)S(1)}, bf16[32,12,3075]{2,1,0:T(8,128)(2,1)S(1)}, s32[]{:T(128)}) while((s32[]{:T(128)}, bf16[32,12,4616]{2,1,0:T(8,128)(2,1)}, s32[32,3]{0,1:T(4,128)S(1)}, bf16[32,12,3075]{2,1,0:T(8,128)(2,1)S(1)}, s32[]{:T(128)}) %tuple.65), condition=%wide.while_cond, body=%wide.while_body.sunk | while | flops 2 | bytes 176317 | solution.py:136
  512.3 93.7 %while.16 = (s32[]{:T(128)}, bf16[32,12,4616]{2,1,0:T(8,128)(2,1)}, s32[32,3]{0,1:T(4,128)S(1)}, bf16[32,12,3075]{2,1,0:T(8,128)(2,1)S(1)}, s32[]{:T(128)}) while((s32[]{:T(128)}, bf16[32,12,4616]{2,1,0:T(8,128)(2,1)}, s32[32,3]{0,1:T(4,128)S(1)}, bf16[32,12,3075]{2,1,0:T(8,128)(2,1)S(1)}, s32[]{:T(128)}) %tuple.65), condition=%wide.while_cond, body=%wide.while_body.sunk | while | flops 2 | bytes 176317 | solution.py:136
  619.9 93.7 %while.16 = (s32[]{:T(128)}, bf16[32,12,4616]{2,1,0:T(8,128)(2,1)}, s32[32,3]{0,1:T(4,128)S(1)}, bf16[32,12,3075]{2,1,0:T(8,128)(2,1)S(1)}, s32[]{:T(128)}) while((s32[]{:T(128)}, bf16[32,12,4616]{2,1,0:T(8,128)(2,1)}, s32[32,3]{0,1:T(4,128)S(1)}, bf16[32,12,3075]{2,1,0:T(8,128)(2,1)S(1)}, s32[]{:T(128)}) %tuple.65), condition=%wide.while_cond, body=%wide.while_body.sunk | while | flops 2 | bytes 176317 | solution.py:136
  (493 shorter events, 462.8 us)
Async XLA Ops:
  6.5 36.1 %all-gather.2.cloned.1.call-start = ((), (), s32[]{:S(2)}) async-start(), calls=%async_computation.1 | async-start | bytes 2949120 | tf_op jit(solution)/shard_map/all_gather | solution.py:120
  7.6 88.8 %copy-start.1 = (f32[3,128]{0,1:T(8,128)}, f32[3,128]{0,1:T(8,128)S(1)}, u32[]{:S(2)}) copy-start(f32[3,128]{0,1:T(8,128)S(1)} %copy.55) | copy-start | bytes 4612
  67.4 29.0 %copy-start.4 = (f32[3,128]{0,1:T(8,128)S(1)}, f32[3,128]{0,1:T(8,128)}, u32[]{:S(2)}) copy-start(f32[3,128]{0,1:T(8,128)} %copy.56) | copy-start | bytes 4612
  96.4 20.4 %slice-start = ((s8[4718592]{0:T(1024)(128)(4,1)}), s8[4194304]{0:T(1024)(128)(4,1)S(1)}, s32[]{:S(2)}) async-start(s8[4718592]{0:T(1024)(128)(4,1)} %bitcast.219), calls=%async_computation.2 | async-start | bytes 8388608
  103.7 3.4 copy-start
  103.8 13.1 %slice-start.1 = ((s8[4718592]{0:T(1024)(128)(4,1)}), s8[524288]{0:T(1024)(128)(4,1)S(1)}, s32[]{:S(2)}) async-start(s8[4718592]{0:T(1024)(128)(4,1)} %bitcast.219), calls=%async_computation.3 | async-start | bytes 1048576
  124.2 12.9 %copy-start.2 = (f32[3,128]{0,1:T(8,128)S(1)}, f32[3,128]{0,1:T(8,128)}, u32[]{:S(2)}) copy-start(f32[3,128]{0,1:T(8,128)} %copy-done.1) | copy-start | bytes 4612
  124.2 12.9 %copy-start.3 = (f32[3,128]{0,1:T(8,128)S(1)}, f32[3,128]{0,1:T(8,128)}, u32[]{:S(2)}) copy-start(f32[3,128]{0,1:T(8,128)} %copy.59) | copy-start | bytes 4612
  137.1 5.6 copy-start.6
  173.7 14.9 %copy-start.5 = (f32[24,128]{1,0:T(8,128)S(1)}, f32[24,128]{1,0:T(8,128)}, u32[]{:S(2)}) copy-start(f32[24,128]{1,0:T(8,128)} %fusion.80) | copy-start | bytes 36868
  220.9 45.1 %all-to-all-start = ((bf16[32,2,18432]{2,1,0:T(2,128)(2,1)}), bf16[32,2,18432]{2,1,0:T(2,128)(2,1)S(1)}, u32[]{:S(2)}, u32[]{:S(2)}) async-start(bf16[32,2,18432]{2,1,0:T(2,128)(2,1)} %reshape.457), calls=%async_computation | async-start | bytes 4718592 | tf_op jit(solution)/shard_map/all_to_all | solution.py:128
Sparse Core Ops, SparseCore 0:
  9.0 33.5 all-gather.1
where the time goes:
time: 749 us; the launch traced here: 734 us
  local copies, waits for them, and re-layouts  479 us (64%)
  matrix products  119 us (16%)
  other arithmetic  60.6 us (8%)
  waiting for transfers between devices  46.2 us (6%)
  between operations  16 us (2%)
  starting transfers between devices  10.1 us (1%)
    gather x384, local copies, waits for them, and re-layouts  372 us
    dot_general x6, matrix products, section(): return jnp.einsum(form, paired, table, precision=product_precision)  90.6 us
    all_to_all x1, waiting for transfers between devices, body(): lax.all_to_all(filtered[None], 'dev', split_axis=1, concat_axis=0, tiled=...  35 us
    dot_general x16, matrix products, one_plane(): jnp.einsum('tyx,t->yx', window[:, :, tap_index:tap_index + W], weight_col...  22.3 us
    all_to_all x2, local copies, waits for them, and re-layouts, body(): lax.all_to_all(filtered[None], 'dev', split_axis=1, concat_axis=0, tiled=...  19 us
    sub x4, other arithmetic, complex_twist(): real_part * twist_cos - imag_part * twist_sin  18.6 us
    neg x1, other arithmetic, response_grid(): return -jnp.sin(chi_scale * focus * radius + phase_shift)  17.1 us
  transfers between devices with their start and end apart: 2, of which 2 were waited for; matrix products, arithmetic and copies ran while one was open for 3% of the time, Pallas kernels for 0%

commit v1 on v0

v1 whole, which is shorter than its diff:
```python
import math

import jax
import jax.numpy as jnp
import ml_dtypes
import numpy as np
from jax import lax
from jax.experimental import pallas as pl
from jax.experimental.pallas import tpu as pltpu
from jax.sharding import PartitionSpec as P

W = 3072
YB = 384
TAPS = 4
TILTS = 32
ZD = 4
XP = 24
XQ = 128
NJ = 12
ROWS = YB // TILTS
TILES = XP * ROWS // 16
LEFT = 6
BLOCKS = 38
GROUP = 4

chi_scale = 200.0
phase_shift = 0.1
root_half = math.sqrt(0.5)
sin_third = math.sqrt(0.75)


def split_np(table):
    high = table.astype(ml_dtypes.bfloat16)
    low = (table - high.astype(np.float64)).astype(ml_dtypes.bfloat16)
    return high, low


def x_tables():
    n2 = np.arange(XQ)
    k2 = np.arange(XQ)
    forward = np.zeros((NJ, 2 * XQ, 2 * XQ))
    inverse = np.zeros((NJ, 2 * XQ, 2 * XQ))
    for j in range(NJ):
        if j == 0:
            for half, k1 in enumerate((0, 12)):
                angle = 2 * np.pi * ((n2[:, None] * (k1 + XP * k2[None, :])) % W) / W
                cas = np.cos(angle) + np.sin(angle)
                cut = slice(half * XQ, (half + 1) * XQ)
                forward[j, cut, cut] = cas
                inverse[j, cut, cut] = cas.T / W
        else:
            angle = 2 * np.pi * ((n2[:, None] * (j + XP * k2[None, :])) % W) / W
            cos, sin = np.cos(angle), np.sin(angle)
            forward[j] = np.block([[cos, -sin], [sin, cos]])
            inverse[j] = np.block([[cos.T, sin.T], [-sin.T, cos.T]]) * (2.0 / W)
    return forward, inverse


def x_frequencies():
    k2 = np.arange(XQ)
    result = np.zeros((NJ, 2 * XQ))
    for j in range(NJ):
        first, second = (0, 12) if j == 0 else (j, j)
        for half, k1 in enumerate((first, second)):
            k = k1 + XP * k2
            result[j, half * XQ : (half + 1) * XQ] = np.where(2 * k < W, k, k - W) / W
    return result


def y_frequencies():
    a = np.arange(YB)
    return np.where(2 * a < YB, a, a - YB) / YB


def row_order():
    first = [ROWS * d + y for d in range(TILTS) for y in range(8)]
    second = [ROWS * d + y for d in range(TILTS) for y in range(8, ROWS)]
    return np.array(first + second)


def y_table():
    a = np.arange(YB)
    angle = 2 * np.pi * ((a[:, None] * a[None, :]) % YB) / YB
    return np.cos(angle) + np.sin(angle)


def real_eight(x):
    s0, d0 = x[0] + x[4], x[0] - x[4]
    s1, d1 = x[1] + x[5], x[1] - x[5]
    s2, d2 = x[2] + x[6], x[2] - x[6]
    s3, d3 = x[3] + x[7], x[3] - x[7]
    t0, t1 = s0 + s2, s1 + s3
    u = (d1 - d3) * root_half
    v = (d1 + d3) * root_half
    return {
        0: (t0 + t1, None),
        4: (t0 - t1, None),
        2: (s0 - s2, s3 - s1),
        1: (d0 + u, -(d2 + v)),
        3: (d0 - u, d2 - v),
    }


def forward_24(x):
    parts = [real_eight([x[(8 * a + 3 * b) % 24] for b in range(8)]) for a in range(3)]
    found = {}

    def put(ka, kb, value):
        for k in range(24):
            if k % 3 == ka % 3 and k % 8 == kb % 8:
                if k <= 12:
                    found[k] = value
                else:
                    re, im = value
                    found[24 - k] = (re, None if im is None else -im)

    for kb in (0, 4):
        p, q, r = (parts[a][kb][0] for a in range(3))
        total = q + r
        put(0, kb, (p + total, None))
        put(1, kb, (p - 0.5 * total, (r - q) * sin_third))
    for kb in (1, 2, 3):
        (pr, pi), (qr, qi), (rr, ri) = (parts[a][kb] for a in range(3))
        tr, ti = qr + rr, qi + ri
        put(0, kb, (pr + tr, pi + ti))
        mr, mi = pr - 0.5 * tr, pi - 0.5 * ti
        er, ei = (qr - rr) * sin_third, (qi - ri) * sin_third
        put(1, kb, (mr + ei, mi - er))
        put(2, kb, (mr - ei, mi + er))
    return found


def inverse_24(v):
    def get(ka, kb):
        k = next(i for i in range(24) if i % 3 == ka and i % 8 == kb)
        if k <= 12:
            return v[k]
        re, im = v[24 - k]
        return (re, -im)

    eights = [dict() for _ in range(3)]
    for kb in (0, 4):
        p = get(0, kb)[0]
        sr, si = get(1, kb)
        m = p - 0.5 * sr
        e = si * sin_third
        eights[0][kb] = (p + sr, None)
        eights[1][kb] = (m - e, None)
        eights[2][kb] = (m + e, None)
    for kb in (1, 2, 3):
        (pr, pi), (qr, qi), (rr, ri) = get(0, kb), get(1, kb), get(2, kb)
        tr, ti = qr + rr, qi + ri
        mr, mi = pr - 0.5 * tr, pi - 0.5 * ti
        er, ei = (qr - rr) * sin_third, (qi - ri) * sin_third
        eights[0][kb] = (pr + tr, pi + ti)
        eights[1][kb] = (mr - ei, mi + er)
        eights[2][kb] = (mr + ei, mi - er)
    out = [None] * 24
    for a in range(3):
        g = eights[a]
        g0, g4 = g[0][0], g[4][0]
        (r1, i1), (r2, i2), (r3, i3) = g[1], g[2], g[3]
        c0, c1 = g0 + g4, g0 - g4
        e0, e2 = c0 + r2, c0 - r2
        o0, o2 = r1 + r3, i1 - i3
        e1, e3 = c1 - i2, c1 + i2
        da, db = (r1 - r3) * root_half, (i1 + i3) * root_half
        o1, o3 = da - db, -(da + db)
        values = [e0 + o0, e1 + o1, e2 - o2, e3 + o3, e0 - o0, e1 - o1, e2 + o2, e3 - o3]
        for b in range(8):
            out[(8 * a + 3 * b) % 24] = values[b]
    return out


def split(value):
    high = value.astype(jnp.bfloat16)
    low = (value - high.astype(jnp.float32)).astype(jnp.bfloat16)
    return high, low


def dot(a, b):
    return jnp.dot(a, b, preferred_element_type=jnp.float32)


STRIP = 16
CHUNK = 128


def filter_kernel(x_ref, fh_ref, fl_ref, ih_ref, il_ref, ah_ref, al_ref, gx_ref, out_ref,
                  vh, vl, uh, ul, back):
    j = pl.program_id(0)

    @pl.when(j == 0)
    def _():
        def strip(i, carry):
            rows = pl.ds(pl.multiple_of(i * STRIP, STRIP), STRIP)
            blocks = [
                x_ref[rows, b * XQ : (b + 1) * XQ].astype(jnp.float32) for b in range(XP)
            ]
            found = forward_24(blocks)
            for jj in range(NJ):
                if jj == 0:
                    pair = (found[0][0], found[12][0])
                else:
                    pair = found[jj]
                for half in range(2):
                    high, low = split(pair[half])
                    vh[jj, rows, half * XQ : (half + 1) * XQ] = high
                    vl[jj, rows, half * XQ : (half + 1) * XQ] = low
            return carry

        lax.fori_loop(0, YB // STRIP, strip, 0)

    for c in range(YB // CHUNK):
        rows = slice(c * CHUNK, (c + 1) * CHUNK)
        high, low = vh[j, rows, :], vl[j, rows, :]
        u = dot(high, fh_ref[0]) + dot(low, fh_ref[0]) + dot(high, fl_ref[0])
        uh[rows, :], ul[rows, :] = split(u)
    gain = gx_ref[0]
    for c in range(YB // CHUNK):
        rows = slice(c * CHUNK, (c + 1) * CHUNK)
        total = None
        for r in range(2):
            cut = slice(r * YB + c * CHUNK, r * YB + (c + 1) * CHUNK)
            y = dot(ah_ref[cut, :], uh[...]) + dot(al_ref[cut, :], uh[...])
            y = y + dot(ah_ref[cut, :], ul[...])
            y = y * gain[r : r + 1, :]
            total = y if total is None else total + y
        high, low = split(total)
        z = dot(high, ih_ref[0]) + dot(low, ih_ref[0]) + dot(high, il_ref[0])
        back[j, rows, :] = z

    def blocks_of(start):
        rows = pl.ds(pl.multiple_of(start, 8), 8)
        v = {}
        for jj in range(NJ):
            first, second = back[jj, rows, 0:XQ], back[jj, rows, XQ : 2 * XQ]
            if jj == 0:
                v[0], v[12] = (first, None), (second, None)
            else:
                v[jj] = (first, second)
        return inverse_24(v)

    @pl.when(j == NJ - 1)
    def _():
        def first_part(d, carry):
            values = blocks_of(d * 8)
            for pair in range(XP // 2):
                tile = jnp.concatenate([values[2 * pair], values[2 * pair + 1]], axis=0)
                out_ref[d, pair] = tile.astype(jnp.bfloat16)
            return carry

        lax.fori_loop(0, TILTS, first_part, 0)

        def second_part(i, carry):
            values = blocks_of(8 * TILTS + i * 8)
            for half in range(2):
                for quad in range(XP // 4):
                    tile = jnp.concatenate(
                        [values[4 * quad + n][4 * half : 4 * half + 4] for n in range(4)], axis=0
                    )
                    out_ref[2 * i + half, XP // 2 + quad] = tile.astype(jnp.bfloat16)
            return carry

        lax.fori_loop(0, TILTS // 2, second_part, 0)


def run_filter(whole, tables, ah, al, gx):
    fh, fl, ih, il = tables
    table_spec = pl.BlockSpec((1, 2 * XQ, 2 * XQ), lambda j: (j, 0, 0))
    return pl.pallas_call(
        filter_kernel,
        grid=(NJ,),
        in_specs=[
            pl.BlockSpec((YB, W), lambda j: (0, 0)),
            table_spec,
            table_spec,
            table_spec,
            table_spec,
            pl.BlockSpec((2 * YB, YB), lambda j: (0, 0)),
            pl.BlockSpec((2 * YB, YB), lambda j: (0, 0)),
            pl.BlockSpec((1, 2, 2 * XQ), lambda j: (j, 0, 0)),
        ],
        out_specs=pl.BlockSpec((TILTS, TILES, 16, XQ), lambda j: (0, 0, 0, 0)),
        out_shape=jax.ShapeDtypeStruct((TILTS, TILES, 16, XQ), jnp.bfloat16),
        scratch_shapes=[
            pltpu.VMEM((NJ, YB, 2 * XQ), jnp.bfloat16),
            pltpu.VMEM((NJ, YB, 2 * XQ), jnp.bfloat16),
            pltpu.VMEM((YB, 2 * XQ), jnp.bfloat16),
            pltpu.VMEM((YB, 2 * XQ), jnp.bfloat16),
            pltpu.VMEM((NJ, YB, 2 * XQ), jnp.float32),
        ],
        compiler_params=pltpu.CompilerParams(
            dimension_semantics=("arbitrary",), vmem_limit_bytes=56 * 2**20
        ),
    )(whole, fh, fl, ih, il, ah, al, gx)


def band_kernel(off_ref, weight_ref, out_ref):
    step = pl.program_id(0)
    distance = lax.broadcasted_iota(jnp.int32, (2 * XQ, XQ), 0) - lax.broadcasted_iota(
        jnp.int32, (2 * XQ, XQ), 1
    )
    for z in range(ZD):
        for g in range(GROUP):
            t = step * GROUP + g
            shift = off_ref[t, z] & (XQ - 1)
            moved = distance - shift
            band = jnp.zeros((2 * XQ, XQ), jnp.float32)
            for tap in range(TAPS):
                band = jnp.where(moved == tap, weight_ref[t, z * TAPS + tap], band)
            out_ref[0, z, g] = band.astype(jnp.bfloat16)


def run_band(off, weights):
    steps = TILTS // GROUP
    return pl.pallas_call(
        band_kernel,
        grid=(steps,),
        in_specs=[
            pl.BlockSpec(memory_space=pltpu.SMEM),
            pl.BlockSpec(memory_space=pltpu.SMEM),
        ],
        out_specs=pl.BlockSpec((1, ZD, GROUP, 2 * XQ, XQ), lambda i: (i, 0, 0, 0, 0)),
        out_shape=jax.ShapeDtypeStruct((steps, ZD, GROUP, 2 * XQ, XQ), jnp.bfloat16),
        compiler_params=pltpu.CompilerParams(dimension_semantics=("arbitrary",)),
    )(off, weights)


def project_kernel(off_ref, weight_ref, x_ref, band_ref, out_ref, padded, total):
    step = pl.program_id(0)

    @pl.when(step == 0)
    def _():
        padded[...] = jnp.zeros_like(padded)
        total[...] = jnp.zeros_like(total)

    for g in range(GROUP):
        for quad in range(XP // 4):
            tail = x_ref[g, XP // 2 + quad].astype(jnp.float32)
            for half in range(2):
                head = x_ref[g, 2 * quad + half].astype(jnp.float32)
                for n in range(2):
                    block = 4 * quad + 2 * half + n
                    part = tail[4 * (2 * half + n) : 4 * (2 * half + n) + 4]
                    tile = jnp.concatenate(
                        [head[8 * n : 8 * n + 8], part, jnp.zeros((4, XQ), jnp.float32)], axis=0
                    )
                    padded[g, LEFT + block] = tile.astype(jnp.bfloat16)

    def window(g, start):
        return padded[g, pl.ds(start, XP)].reshape(XP * 16, XQ)

    for z in range(ZD):
        parts = []
        for g in range(GROUP):
            start = (off_ref[step * GROUP + g, z] >> 7) + LEFT
            parts.append(window(g, start))
            parts.append(window(g, start + 1))
        left = jnp.concatenate(parts, axis=1)
        band = band_ref[0, z].reshape(GROUP * 2 * XQ, XQ)
        total[z] += dot(left, band)

    for g in range(GROUP):
        t = step * GROUP + g
        for z in range(ZD):
            shift = off_ref[t, z] & (XQ - 1)

            @pl.when(shift > XQ - TAPS + 1)
            def _():
                moved = (
                    lax.broadcasted_iota(jnp.int32, (XQ, XQ), 0)
                    - lax.broadcasted_iota(jnp.int32, (XQ, XQ), 1)
                    + (2 * XQ - shift)
                )
                band = jnp.zeros((XQ, XQ), jnp.float32)
                for tap in range(TAPS):
                    band = jnp.where(moved == tap, weight_ref[t, z * TAPS + tap], band)
                start = (off_ref[t, z] >> 7) + LEFT
                total[z] += dot(window(g, start + 2), band.astype(jnp.bfloat16))

    @pl.when(step == pl.num_programs(0) - 1)
    def _():
        for z in range(ZD):
            for b in range(XP):
                out_ref[:, z, b * XQ : (b + 1) * XQ] = total[z, b * 16 : b * 16 + ROWS, :]


def run_project(off, weights, moved, bands):
    steps = TILTS // GROUP
    return pl.pallas_call(
        project_kernel,
        grid=(steps,),
        in_specs=[
            pl.BlockSpec(memory_space=pltpu.SMEM),
            pl.BlockSpec(memory_space=pltpu.SMEM),
            pl.BlockSpec((GROUP, TILES, 16, XQ), lambda i: (i, 0, 0, 0)),
            pl.BlockSpec((1, ZD, GROUP, 2 * XQ, XQ), lambda i: (i, 0, 0, 0, 0)),
        ],
        out_specs=pl.BlockSpec((ROWS, ZD, W), lambda i: (0, 0, 0)),
        out_shape=jax.ShapeDtypeStruct((ROWS, ZD, W), jnp.float32),
        scratch_shapes=[
            pltpu.VMEM((GROUP, BLOCKS, 16, XQ), jnp.bfloat16),
            pltpu.VMEM((ZD, XP * 16, XQ), jnp.float32),
        ],
        compiler_params=pltpu.CompilerParams(
            dimension_semantics=("arbitrary",), vmem_limit_bytes=48 * 2**20
        ),
    )(off, weights, moved, bands)


def responses(focus):
    scale = chi_scale * focus
    fy = jnp.asarray(y_frequencies(), jnp.float32)
    angle_y = scale * (fy * fy) + phase_shift
    fx = jnp.asarray(x_frequencies(), jnp.float32)
    angle_x = scale * (fx * fx)
    table = y_table()
    left = jnp.asarray(table[row_order()] / YB, jnp.float32)
    right = jnp.asarray(table, jnp.float32)
    side = jnp.concatenate([left * -jnp.sin(angle_y), left * -jnp.cos(angle_y)], axis=0)
    mixed = jnp.dot(side, right, precision=lax.Precision.HIGHEST)
    rounded = lax.reduce_precision(mixed, exponent_bits=8, mantissa_bits=7)
    ah, al = rounded.astype(jnp.bfloat16), (mixed - rounded).astype(jnp.bfloat16)
    gx = jnp.stack([jnp.cos(angle_x), jnp.sin(angle_x)], axis=1)
    return ah, al, gx


def body(tilts, tilt_defocus, defocus_table, slab_pick, interp_offset, interp_weights):
    entries = jnp.arange(defocus_table.shape[0], dtype=jnp.int32)
    group_defocus = jnp.sum(jnp.where(entries == slab_pick[0], defocus_table, 0.0))
    focus = tilt_defocus[0] + group_defocus
    whole = lax.all_gather(tilts, "slab", axis=1, tiled=True)
    ah, al, gx = responses(focus)
    weights = interp_weights.astype(jnp.float32).reshape(TILTS, ZD * TAPS)
    bands = run_band(interp_offset, weights)
    forward, inverse = x_tables()
    tables = [jnp.asarray(t) for pair in (split_np(forward), split_np(inverse)) for t in pair]
    filtered = run_filter(whole[0], tables, ah, al, gx)
    moved = lax.all_to_all(filtered, "dev", split_axis=0, concat_axis=0, tiled=True)
    return run_project(interp_offset, weights, moved, bands)


def solution(mesh):
    in_specs = (
        P("dev", "slab", None),
        P("dev"),
        P(),
        P("slab"),
        P(None, "slab"),
        P(None, "slab", None),
    )
    out_specs = P("dev", "slab", None)
    return jax.shard_map(body, mesh=mesh, in_specs=in_specs, out_specs=out_specs, check_vma=False)
```

time: 749 us -> 135 us (0.18); the launches traced: 734 us -> 134 us
  local copies, waits for them, and re-layouts: 479 us -> 1.41 us
  matrix products: 119 us -> 3.34 us
  other arithmetic: 60.6 us -> 4.56 us
  Pallas kernels: 0 us -> 48.8 us
    gather x384 -> x0, local copies, waits for them, and re-layouts: 372 us -> none
    dot_general x24 -> x1, matrix products: 119 us -> 3.34 us  [responses(): mixed = jnp.dot(side, right, precision=lax.Precision.HIGHEST)]
    pallas_call x0 -> x3, Pallas kernels: none -> 48.8 us  [the longest x1 27.6 us: run_filter(): pl.pallas_call(filter_kernel, grid=(NJ,), in_specs=[pl.BlockSpec((YB, W),...]
    all_to_all x2 -> x0, local copies, waits for them, and re-layouts: 19 us -> none  [body(): lax.all_to_all(filtered[None], 'dev', split_axis=1, concat_axis=0, tiled=...]
    sub x4 -> x0, other arithmetic: 18.6 us -> none  [complex_twist(): real_part * twist_cos - imag_part * twist_sin]
    neg x3 -> x1, other arithmetic: 17.2 us -> 0.72 us  [responses(): -jnp.sin(angle_y)]
    all_gather x1, waiting for transfers between devices: 10.5 us -> 25.4 us  [body(): whole = lax.all_gather(tilts, 'slab', axis=1, tiled=True)]
    dynamic_update_slice x8 -> x0, local copies, waits for them, and re-layouts: 14.6 us -> none  [body(): lax.map(one_plane, (interp_offset.T, jnp.swapaxes(interp_weights, 0, 1)))]
  transfers between devices with their start and end apart: 2 -> 2, of which waited for: 2 -> 2; matrix products, arithmetic and copies ran while one was open for 3% -> 7% of each run, Pallas kernels for 0% -> 6%
where the time goes in v1:
time: 135 us; the launch traced here: 134 us
  waiting for transfers between devices  51.2 us (38%)
  Pallas kernels  48.8 us (36%)
  between operations  15.4 us (11%)
  starting transfers between devices  9.86 us (7%)
  other arithmetic  4.56 us (3%)
  matrix products  3.34 us (2%)
  local copies, waits for them, and re-layouts  1.41 us (1%)
    pallas_call x1, Pallas kernels, run_filter(): pl.pallas_call(filter_kernel, grid=(NJ,), in_specs=[pl.BlockSpec((YB, W),...  27.6 us
    all_gather x1, waiting for transfers between devices, body(): whole = lax.all_gather(tilts, 'slab', axis=1, tiled=True)  25.4 us
    all_to_all x1, waiting for transfers between devices, body(): lax.all_to_all(filtered, 'dev', split_axis=0, concat_axis=0, tiled=True)  25.1 us
    pallas_call x1, Pallas kernels, run_project(): pl.pallas_call(project_kernel, grid=(steps,), in_specs=[pl.BlockSpec(memo...  12.5 us
    all_to_all x1, starting transfers between devices, body(): lax.all_to_all(filtered, 'dev', split_axis=0, concat_axis=0, tiled=True)  9.86 us
    pallas_call x1, Pallas kernels, run_band(): pl.pallas_call(band_kernel, grid=(steps,), in_specs=[pl.BlockSpec(memory_...  8.69 us
    dot_general x1, matrix products, responses(): mixed = jnp.dot(side, right, precision=lax.Precision.HIGHEST)  3.34 us
  transfers between devices with their start and end apart: 2, of which 2 were waited for; matrix products, arithmetic and copies ran while one was open for 7% of the time, Pallas kernels for 6%

profile of v1, /device:TPU:2, one launch (start us, length us, event | category | flops | bytes accessed | tf_op | source)
XLA Modules:
  0.0 134.5 jit_solution(11102588332792712321)
XLA Ops:
  6.5 0.0 copy-start.2
  6.5 0.0 all-gather.2.cloned.1.call-start
  6.5 0.7 all-gather.2.cloned.1.call-update
  8.5 1.3 fusion.6
  10.5 0.8 fusion.5
  11.3 0.6 pad_maximum_fusion.gx_ref
  11.9 0.7 sine_negate_fusion
  12.6 1.1 broadcast_multiply_fusion.1
  13.8 0.0 copy-done.2
  13.8 3.3 %fusion = (bf16[768,384]{1,0:T(8,128)(2,1)}, bf16[768,384]{1,0:T(8,128)(2,1)}) fusion(f32[384,384]{1,0:T(8,128)S(1)} %copy-done.2, f32[384,384]{1,0:T(8,128)S(1)} %get-tuple-element.8, f32[384,384]{1,0:T(8,128)S(1)} %get-tuple-element.7), kind=kOutput, calls=%fused_computation.2 | convolution fusion | flops 1360429056 | bytes 2949120 | tf_op jit(solution)/shard_map/dot_general | solution.py:422
  17.1 25.4 %all-gather.2.cloned.1.call-done = bf16[1,384,3072]{2,1,0:T(8,128)(2,1)} async-done(((bf16[1,96,3072]{2,1,0:T(8,128)(2,1)}), bf16[1,384,3072]{2,1,0:T(8,128)(2,1)}) %all-gather.2.cloned.1.call-update) | async-done | bytes 2359312 | tf_op jit(solution)/shard_map/all_gather | solution.py:433
  42.5 27.6 %shard_map.136 = bf16[32,18,16,128]{3,2,1,0:T(8,128)(2,1)} custom-call(bf16[384,3072]{1,0:T(8,128)(2,1)} %bitcast.10, bf16[12,256,256]{2,1,0:T(8,128)(2,1)} %constant.26.clone.fh_ref, bf16[12,256,256]{2,1,0:T(8,128)(2,1)} %constant.27.clone.fl_ref, bf16[12,256,256]{2,1,0:T(8,128)(2,1)} %constant.28.clone.ih_ref, ...), custom_call_target="tpu_custom_call" | custom-call | tf_op jit(solution)/shard_map/pallas_call | solution.py:271
  70.2 0.0 copy-start.4
  70.2 0.0 copy-start.3
  70.2 9.9 %all-to-all-start = ((bf16[32,18,16,128]{3,2,1,0:T(8,128)(2,1)}), bf16[32,18,16,128]{3,2,1,0:T(8,128)(2,1)S(1)}, u32[]{:S(2)}, u32[]{:S(2)}) async-start(bf16[32,18,16,128]{3,2,1,0:T(8,128)(2,1)} %shard_map.136), calls=%async_computation | async-start | bytes 4718592 | tf_op jit(solution)/shard_map/all_to_all | solution.py:440
  80.0 0.0 copy-done.4
  80.0 0.7 copy.22.off_ref
  80.7 0.0 copy-done.3
  80.7 0.7 copy.23.weight_ref
  81.4 8.7 %shard_map.137.band_ref = bf16[8,4,4,256,128]{4,3,2,1,0:T(8,128)(2,1)} custom-call(s32[32,4]{1,0:T(8,128)} %copy.22.off_ref, f32[32,16]{1,0:T(8,128)} %copy.23.weight_ref), custom_call_target="tpu_custom_call" | custom-call | tf_op jit(solution)/shard_map/pallas_call | solution.py:317
  90.1 25.1 %all-to-all-done.x_ref = bf16[32,18,16,128]{3,2,1,0:T(8,128)(2,1)S(1)} async-done(((bf16[32,18,16,128]{3,2,1,0:T(8,128)(2,1)}), bf16[32,18,16,128]{3,2,1,0:T(8,128)(2,1)S(1)}, u32[]{:S(2)}, u32[]{:S(2)}) %all-to-all-start) | async-done | bytes 2359328 | tf_op jit(solution)/shard_map/all_to_all | solution.py:440
  115.2 0.0 copy-done
  115.2 0.0 copy-done.1
  115.2 12.5 %shard_map.138 = f32[12,4,3072]{2,1,0:T(4,128)} custom-call(s32[32,4]{1,0:T(8,128)S(1)} %copy-done.1, f32[32,16]{1,0:T(8,128)S(1)} %copy-done, bf16[32,18,16,128]{3,2,1,0:T(8,128)(2,1)S(1)} %all-to-all-done.x_ref, bf16[8,4,4,256,128]{4,3,2,1,0:T(8,128)(2,1)} %shard_map.137.band_ref), custom_call_target="tpu_custom_call" | custom-call | tf_op jit(solution)/shard_map/pallas_call | solution.py:391
  (4 shorter events, 0.0 us)
Async XLA Ops:
  6.5 7.3 %copy-start.2 = (f32[384,384]{1,0:T(8,128)S(1)}, f32[384,384]{1,0:T(8,128)}, u32[]{:S(2)}) copy-start(f32[384,384]{1,0:T(8,128)} %constant.25.clone) | copy-start | bytes 1769476
  6.5 36.0 %all-gather.2.cloned.1.call-start = ((), (), s32[]{:S(2)}) async-start(), calls=%async_computation.1 | async-start | bytes 2949120 | tf_op jit(solution)/shard_map/all_gather | solution.py:433
  70.2 9.9 %copy-start.4 = (s32[32,4]{0,1:T(4,128)S(1)}, s32[32,4]{0,1:T(4,128)}, u32[]{:S(2)}) copy-start(s32[32,4]{0,1:T(4,128)} %param.18) | copy-start | bytes 1540
  70.2 10.6 %copy-start.3 = (bf16[32,4,4]{0,2,1:T(4,128)(2,1)S(1)}, bf16[32,4,4]{0,2,1:T(4,128)(2,1)}, u32[]{:S(2)}) copy-start(bf16[32,4,4]{0,2,1:T(4,128)(2,1)} %param.19) | copy-start | bytes 3076
  70.2 45.0 %all-to-all-start = ((bf16[32,18,16,128]{3,2,1,0:T(8,128)(2,1)}), bf16[32,18,16,128]{3,2,1,0:T(8,128)(2,1)S(1)}, u32[]{:S(2)}, u32[]{:S(2)}) async-start(bf16[32,18,16,128]{3,2,1,0:T(8,128)(2,1)} %shard_map.136), calls=%async_computation | async-start | bytes 4718592 | tf_op jit(solution)/shard_map/all_to_all | solution.py:440
  81.4 33.8 %copy-start = (f32[32,16]{1,0:T(8,128)S(1)}, f32[32,16]{1,0:T(8,128)}, u32[]{:S(2)}) copy-start(f32[32,16]{1,0:T(8,128)} %copy.23.weight_ref) | copy-start | bytes 6148
  81.4 33.8 %copy-start.1 = (s32[32,4]{1,0:T(8,128)S(1)}, s32[32,4]{1,0:T(8,128)}, u32[]{:S(2)}) copy-start(s32[32,4]{1,0:T(8,128)} %copy.22.off_ref) | copy-start | bytes 1540
Sparse Core Ops, SparseCore 0:
  9.0 33.4 all-gather.1

commit v2 on v1

v2 whole, which is shorter than its diff:
```python
import math

import jax
import jax.numpy as jnp
import ml_dtypes
import numpy as np
from jax import lax
from jax.experimental import pallas as pl
from jax.experimental.pallas import tpu as pltpu
from jax.sharding import PartitionSpec as P

W = 3072
YB = 384
TAPS = 4
TILTS = 32
ZD = 4
XP = 24
XQ = 128
NJ = 12
ROWS = YB // TILTS
PARTS = ((0, 8), (8, 4))
TILES = XP * ROWS // 16
HALF = YB // 2
QUARTER = YB // 4
DEPTH = 256
LEFT = 8
SPAN = 40
GROUP = 4

chi_scale = 200.0
phase_shift = 0.1
root_half = math.sqrt(0.5)
sin_third = math.sqrt(0.75)


def split_np(table):
    high = table.astype(ml_dtypes.bfloat16)
    low = (table - high.astype(np.float64)).astype(ml_dtypes.bfloat16)
    return high, low


def x_tables():
    n2 = np.arange(XQ)
    k2 = np.arange(XQ)
    forward = np.zeros((NJ, 2 * XQ, 2 * XQ))
    inverse = np.zeros((NJ, 2 * XQ, 2 * XQ))
    for j in range(NJ):
        if j == 0:
            for half, k1 in enumerate((0, 12)):
                angle = 2 * np.pi * ((n2[:, None] * (k1 + XP * k2[None, :])) % W) / W
                cas = np.cos(angle) + np.sin(angle)
                cut = slice(half * XQ, (half + 1) * XQ)
                forward[j, cut, cut] = cas
                inverse[j, cut, cut] = cas.T / W
        else:
            angle = 2 * np.pi * ((n2[:, None] * (j + XP * k2[None, :])) % W) / W
            cos, sin = np.cos(angle), np.sin(angle)
            forward[j] = np.block([[cos, -sin], [sin, cos]])
            inverse[j] = np.block([[cos.T, sin.T], [-sin.T, cos.T]]) * (2.0 / W)
    return forward, inverse


def x_frequencies():
    k2 = np.arange(XQ)
    result = np.zeros((NJ, 2 * XQ))
    for j in range(NJ):
        first, second = (0, 12) if j == 0 else (j, j)
        for half, k1 in enumerate((first, second)):
            k = k1 + XP * k2
            result[j, half * XQ : (half + 1) * XQ] = np.where(2 * k < W, k, k - W) / W
    return result


def y_frequencies():
    a = np.arange(YB)
    return np.where(2 * a < YB, a, a - YB) / YB


def y_tables():
    y = np.arange(HALF)
    wanted = np.array(
        [
            ROWS * d + first + i
            for first, count in PARTS
            for d in range(TILTS // 2)
            for i in range(count)
        ]
    )
    left, right = [], []
    for odd in range(2):
        a = np.arange(odd, YB, 2)

        def cas(rows):
            angle = 2 * np.pi * ((rows[:, None] * a[None, :]) % YB) / YB
            return np.cos(angle) + np.sin(angle)

        left.append(cas(wanted) / YB)
        given = cas(y).T
        swapped = np.concatenate([given[:, QUARTER:], given[:, :QUARTER]], axis=1)
        right.append([given, swapped])
    return np.array(left, np.float32), np.array(right, np.float32)


def real_eight(x):
    s0, d0 = x[0] + x[4], x[0] - x[4]
    s1, d1 = x[1] + x[5], x[1] - x[5]
    s2, d2 = x[2] + x[6], x[2] - x[6]
    s3, d3 = x[3] + x[7], x[3] - x[7]
    t0, t1 = s0 + s2, s1 + s3
    u = (d1 - d3) * root_half
    v = (d1 + d3) * root_half
    return {
        0: (t0 + t1, None),
        4: (t0 - t1, None),
        2: (s0 - s2, s3 - s1),
        1: (d0 + u, -(d2 + v)),
        3: (d0 - u, d2 - v),
    }


def forward_24(x):
    parts = [real_eight([x[(8 * a + 3 * b) % 24] for b in range(8)]) for a in range(3)]
    found = {}

    def put(ka, kb, value):
        for k in range(24):
            if k % 3 == ka % 3 and k % 8 == kb % 8:
                if k <= 12:
                    found[k] = value
                else:
                    re, im = value
                    found[24 - k] = (re, None if im is None else -im)

    for kb in (0, 4):
        p, q, r = (parts[a][kb][0] for a in range(3))
        total = q + r
        put(0, kb, (p + total, None))
        put(1, kb, (p - 0.5 * total, (r - q) * sin_third))
    for kb in (1, 2, 3):
        (pr, pi), (qr, qi), (rr, ri) = (parts[a][kb] for a in range(3))
        tr, ti = qr + rr, qi + ri
        put(0, kb, (pr + tr, pi + ti))
        mr, mi = pr - 0.5 * tr, pi - 0.5 * ti
        er, ei = (qr - rr) * sin_third, (qi - ri) * sin_third
        put(1, kb, (mr + ei, mi - er))
        put(2, kb, (mr - ei, mi + er))
    return found


def inverse_24(v):
    def get(ka, kb):
        k = next(i for i in range(24) if i % 3 == ka and i % 8 == kb)
        if k <= 12:
            return v[k]
        re, im = v[24 - k]
        return (re, -im)

    eights = [dict() for _ in range(3)]
    for kb in (0, 4):
        p = get(0, kb)[0]
        sr, si = get(1, kb)
        m = p - 0.5 * sr
        e = si * sin_third
        eights[0][kb] = (p + sr, None)
        eights[1][kb] = (m - e, None)
        eights[2][kb] = (m + e, None)
    for kb in (1, 2, 3):
        (pr, pi), (qr, qi), (rr, ri) = get(0, kb), get(1, kb), get(2, kb)
        tr, ti = qr + rr, qi + ri
        mr, mi = pr - 0.5 * tr, pi - 0.5 * ti
        er, ei = (qr - rr) * sin_third, (qi - ri) * sin_third
        eights[0][kb] = (pr + tr, pi + ti)
        eights[1][kb] = (mr - ei, mi + er)
        eights[2][kb] = (mr + ei, mi - er)
    out = [None] * 24
    for a in range(3):
        g = eights[a]
        g0, g4 = g[0][0], g[4][0]
        (r1, i1), (r2, i2), (r3, i3) = g[1], g[2], g[3]
        c0, c1 = g0 + g4, g0 - g4
        e0, e2 = c0 + r2, c0 - r2
        o0, o2 = r1 + r3, i1 - i3
        e1, e3 = c1 - i2, c1 + i2
        da, db = (r1 - r3) * root_half, (i1 + i3) * root_half
        o1, o3 = da - db, -(da + db)
        values = [e0 + o0, e1 + o1, e2 - o2, e3 + o3, e0 - o0, e1 - o1, e2 + o2, e3 - o3]
        for b in range(8):
            out[(8 * a + 3 * b) % 24] = values[b]
    return out


def split(value):
    high = value.astype(jnp.bfloat16)
    low = (value - high.astype(jnp.float32)).astype(jnp.bfloat16)
    return high, low


def three_products(high, low, table_high, table_low):
    left = jnp.concatenate([high, low, high], axis=1)
    right = jnp.concatenate([table_high, table_high, table_low], axis=0)
    return jnp.dot(left, right, preferred_element_type=jnp.float32)


STRIP = 16


def load_strips(x_refs, vh, vl):
    for n, x_ref in enumerate(x_refs):

        def strip(i, carry):
            rows = pl.ds(pl.multiple_of(i * STRIP, STRIP), STRIP)
            target = pl.ds(pl.multiple_of(n * QUARTER + i * STRIP, STRIP), STRIP)
            blocks = [
                x_ref[rows, b * XQ : (b + 1) * XQ].astype(jnp.float32) for b in range(XP)
            ]
            found = forward_24(blocks)
            for jj in range(NJ):
                if jj == 0:
                    pair = (found[0][0], found[12][0])
                else:
                    pair = found[jj]
                for half in range(2):
                    high, low = split(pair[half])
                    vh[jj, target, half * XQ : (half + 1) * XQ] = high
                    vl[jj, target, half * XQ : (half + 1) * XQ] = low
            return carry

        lax.fori_loop(0, QUARTER // STRIP, strip, 0)


def near_kernel(focus_ref, slab_ref, xa_ref, xb_ref, fh_ref, fl_ref, left_ref, right_ref, fy_ref,
                fx_ref, out_ref, mix_ref, gain_ref, vh, vl):
    load_strips((xa_ref, xb_ref), vh, vl)

    def column(j, carry):
        out_ref[j] = three_products(vh[j], vl[j], fh_ref[j], fl_ref[j])
        return carry

    lax.fori_loop(0, NJ, column, 0)
    scale = chi_scale * focus_ref[0]
    slab = slab_ref[0]
    angle_x = scale * (fx_ref[...] * fx_ref[...])
    cos_x, sin_x = jnp.cos(angle_x), jnp.sin(angle_x)
    for j in range(NJ):
        gain_ref[j] = jnp.concatenate([cos_x[j : j + 1], sin_x[j : j + 1]], axis=0)
    for odd in range(2):
        fy = fy_ref[odd : odd + 1, :]
        angle_y = scale * (fy * fy) + phase_shift
        left = left_ref[odd]
        side = jnp.concatenate([left * -jnp.sin(angle_y), left * -jnp.cos(angle_y)], axis=0)
        right = right_ref[odd, slab & 1]
        mixed = jnp.dot(
            side, right, precision=lax.Precision.HIGHEST, preferred_element_type=jnp.float32
        )
        if odd:
            mixed = mixed * jnp.where(slab < 2, 1.0, -1.0)
        empty = jnp.zeros((YB, DEPTH - HALF), jnp.float32)
        high, low = split(jnp.concatenate([mixed, empty], axis=1))
        mix_ref[odd] = jnp.concatenate([high, low, high], axis=1)


def parameters():
    return pltpu.CompilerParams(vmem_limit_bytes=63 * 2**20)


def scalar_spec():
    return pl.BlockSpec(memory_space=pltpu.SMEM)


def halves():
    return [pltpu.VMEM((NJ, HALF, 2 * XQ), jnp.bfloat16)] * 2


def run_near(focus, slab, xa, xb, fh, fl):
    left, right = y_tables()
    fy = y_frequencies()
    fy = np.stack([fy[0::2], fy[1::2]]).astype(np.float32)
    fx = x_frequencies().astype(np.float32)
    return pl.pallas_call(
        near_kernel,
        in_specs=[scalar_spec()] * 2 + [pl.BlockSpec(memory_space=pltpu.VMEM)] * 8,
        out_shape=[
            jax.ShapeDtypeStruct((NJ, HALF, 2 * XQ), jnp.float32),
            jax.ShapeDtypeStruct((2, YB, 3 * DEPTH), jnp.bfloat16),
            jax.ShapeDtypeStruct((NJ, 2, 2 * XQ), jnp.float32),
        ],
        scratch_shapes=halves(),
        compiler_params=parameters(),
        name="near",
    )(focus, slab, xa, xb, fh, fl, *(jnp.asarray(t) for t in (left, right, fy, fx)))


def main_kernel(xa_any, xb_any, near_any, fh_any, fl_any, mix_any, gain_any, ih_any, il_any,
                out_any, xa, xb, near, fh, fl, mix, gain, ih, il, vh, vl, back, out,
                early, late, sent):
    first = [(xa_any, xa), (xb_any, xb), (mix_any, mix), (gain_any, gain)]
    copies = [pltpu.make_async_copy(a, b, early.at[i]) for i, (a, b) in enumerate(first)]
    for copy in copies[:2]:
        copy.start()
    streams = [(near_any, near), (fh_any, fh), (fl_any, fl), (ih_any, ih), (il_any, il)]

    def stream(n, j):
        source, target = streams[n]
        return pltpu.make_async_copy(source.at[j], target.at[j], late.at[n, j])

    for j in range(NJ):
        for n in range(len(streams)):
            stream(n, j).start()
        if j == 0:
            for copy in copies[2:]:
                copy.start()
    for copy in copies[:2]:
        copy.wait()
    load_strips((xa, xb), vh, vl)
    for copy in copies[2:]:
        copy.wait()
    empty = jnp.zeros((DEPTH - HALF, 2 * XQ), jnp.bfloat16)

    def column(j, carry):
        for n in range(len(streams)):
            stream(n, j).wait()
        far = three_products(vh[j], vl[j], fh[j], fl[j])
        here = near[j]
        factors = gain[j]

        def mixed(odd, value):
            high, low = split(value)
            right = jnp.concatenate([high, empty, high, empty, low, empty], axis=0)
            y = jnp.dot(mix[odd], right, preferred_element_type=jnp.float32)
            return y[:HALF] * factors[0:1] + y[HALF:] * factors[1:2]

        even = mixed(0, here + far)
        odd = mixed(1, here - far)
        high, low = split(jnp.concatenate([even + odd, even - odd], axis=0))
        back[j] = three_products(high, low, ih[j], il[j])
        return carry

    lax.fori_loop(0, NJ, column, 0)

    def blocks_of(start):
        cut = pl.ds(pl.multiple_of(start, 8), 8)
        v = {}
        for jj in range(NJ):
            one, two = back[jj, cut, 0:XQ], back[jj, cut, XQ : 2 * XQ]
            if jj == 0:
                v[0], v[12] = (one, None), (two, None)
            else:
                v[jj] = (one, two)
        return inverse_24(v)

    devices = TILTS // 2
    for half in range(2):
        low_row, low_tile = half * HALF, 0
        for _, count in PARTS:
            per_strip, per_tile = 8 // count, 16 // count

            def strip(i, carry):
                values = blocks_of(low_row + i * 8)
                for part in range(per_strip):
                    cut = slice(part * count, (part + 1) * count)
                    for tile in range(XP // per_tile):
                        pieces = [values[per_tile * tile + n][cut] for n in range(per_tile)]
                        joined = jnp.concatenate(pieces, axis=0)
                        place = half * devices + i * per_strip + part
                        out[place, low_tile + tile] = joined.astype(jnp.bfloat16)
                return carry

            lax.fori_loop(0, devices // per_strip, strip, 0)
            low_row += devices * count
            low_tile += XP // per_tile
        cut = pl.ds(half * devices, devices)
        pltpu.make_async_copy(out.at[cut], out_any.at[cut], sent.at[half]).start()
    for half in range(2):
        cut = pl.ds(half * devices, devices)
        pltpu.make_async_copy(out.at[cut], out_any.at[cut], sent.at[half]).wait()


def run_main(xa, xb, near, mix, gain, fh, fl, ih, il):
    shape = (TILTS, TILES, 16, XQ)
    args = (xa, xb, near, fh, fl, mix, gain, ih, il)
    return pl.pallas_call(
        main_kernel,
        in_specs=[pl.BlockSpec(memory_space=pl.ANY)] * len(args),
        out_specs=pl.BlockSpec(memory_space=pl.ANY),
        out_shape=jax.ShapeDtypeStruct(shape, jnp.bfloat16),
        scratch_shapes=[pltpu.VMEM(a.shape, a.dtype) for a in args]
        + halves()
        + [
            pltpu.VMEM((NJ, YB, 2 * XQ), jnp.float32),
            pltpu.VMEM(shape, jnp.bfloat16),
            pltpu.SemaphoreType.DMA((4,)),
            pltpu.SemaphoreType.DMA((5, NJ)),
            pltpu.SemaphoreType.DMA((2,)),
        ],
        compiler_params=parameters(),
        name="main",
    )(*args)


def band_kernel(off_ref, weight_ref, out_ref):
    step = pl.program_id(0)
    distance = lax.broadcasted_iota(jnp.int32, (2 * XQ, XQ), 0) - lax.broadcasted_iota(
        jnp.int32, (2 * XQ, XQ), 1
    )
    for z in range(ZD):
        for g in range(GROUP):
            t = step * GROUP + g
            shift = off_ref[t, z] & (XQ - 1)
            moved = distance - shift
            band = jnp.zeros((2 * XQ, XQ), jnp.float32)
            for tap in range(TAPS):
                band = jnp.where(moved == tap, weight_ref[t, z * TAPS + tap], band)
            out_ref[0, z, g] = band.astype(jnp.bfloat16)


def run_band(off, weights):
    steps = TILTS // GROUP
    return pl.pallas_call(
        band_kernel,
        grid=(steps,),
        in_specs=[
            pl.BlockSpec(memory_space=pltpu.SMEM),
            pl.BlockSpec(memory_space=pltpu.SMEM),
        ],
        out_specs=pl.BlockSpec((1, ZD, GROUP, 2 * XQ, XQ), lambda i: (i, 0, 0, 0, 0)),
        out_shape=jax.ShapeDtypeStruct((steps, ZD, GROUP, 2 * XQ, XQ), jnp.bfloat16),
        compiler_params=pltpu.CompilerParams(dimension_semantics=("arbitrary",)),
    )(off, weights)


def project_kernel(off_ref, weight_ref, x_any, band_any, out_ref, x, bands, arrived, wide, narrow,
                   total):
    steps = TILTS // GROUP

    def fetch(i):
        some = pl.ds(i * GROUP, GROUP)
        return (
            pltpu.make_async_copy(x_any.at[some], x.at[some], arrived.at[0, i]),
            pltpu.make_async_copy(band_any.at[i], bands.at[i], arrived.at[1, i]),
        )

    for i in range(steps):
        for copy in fetch(i):
            copy.start()
    wide[...] = jnp.zeros_like(wide)
    narrow[...] = jnp.zeros_like(narrow)
    total[...] = jnp.zeros_like(total)
    layouts = []
    base = 0
    for padded, (_, count) in zip((wide, narrow), PARTS):
        per_tile = 16 // count
        layouts.append((padded, count, per_tile, XP // per_tile, base))
        base += XP // per_tile

    def window(g, start):
        pieces = []
        for padded, count, per_tile, tiles, _ in layouts:
            log_tile = per_tile.bit_length() - 1
            piece = padded[start & (per_tile - 1), g, pl.ds(start >> log_tile, tiles)]
            pieces.append(piece.reshape(tiles * 16, XQ))
        return jnp.concatenate(pieces, axis=0)

    def step(i, carry):
        for copy in fetch(i):
            copy.wait()
        for g in range(GROUP):
            t = i * GROUP + g
            for padded, count, per_tile, tiles, base in layouts:
                lead = LEFT // per_tile
                rows = [x[t, base + p].astype(jnp.float32) for p in range(tiles)]
                empty = jnp.zeros((16, XQ), jnp.float32)
                for p in range(tiles):
                    padded[0, g, lead + p] = x[t, base + p]
                for m in range(1, per_tile):
                    for p in range(-1, tiles):
                        here = rows[p] if p >= 0 else empty
                        later = rows[p + 1] if p + 1 < tiles else empty
                        tile = jnp.concatenate([here[m * count :], later[: m * count]], axis=0)
                        padded[m, g, lead + p] = tile.astype(jnp.bfloat16)
        for z in range(ZD):
            parts = []
            for g in range(GROUP):
                start = (off_ref[i * GROUP + g, z] >> 7) + LEFT
                parts.append(window(g, start))
                parts.append(window(g, start + 1))
            left = jnp.concatenate(parts, axis=1)
            band = bands[i, z].reshape(GROUP * 2 * XQ, XQ)
            total[z] += jnp.dot(left, band, preferred_element_type=jnp.float32)

        for g in range(GROUP):
            t = i * GROUP + g
            for z in range(ZD):
                shift = off_ref[t, z] & (XQ - 1)

                @pl.when(shift > XQ - TAPS + 1)
                def _():
                    moved = (
                        lax.broadcasted_iota(jnp.int32, (XQ, XQ), 0)
                        - lax.broadcasted_iota(jnp.int32, (XQ, XQ), 1)
                        + (2 * XQ - shift)
                    )
                    band = jnp.zeros((XQ, XQ), jnp.float32)
                    for tap in range(TAPS):
                        band = jnp.where(moved == tap, weight_ref[t, z * TAPS + tap], band)
                    start = (off_ref[t, z] >> 7) + LEFT
                    total[z] += jnp.dot(
                        window(g, start + 2),
                        band.astype(jnp.bfloat16),
                        preferred_element_type=jnp.float32,
                    )

        return carry

    lax.fori_loop(0, steps, step, 0)
    for z in range(ZD):
        for (first, count), (_, _, _, _, base) in zip(PARTS, layouts):
            for b in range(XP):
                row = base * 16 + b * count
                out_ref[first : first + count, z, b * XQ : (b + 1) * XQ] = total[
                    z, row : row + count, :
                ]


def run_project(off, weights, moved, bands):
    steps = TILTS // GROUP
    return pl.pallas_call(
        project_kernel,
        in_specs=[scalar_spec()] * 2 + [pl.BlockSpec(memory_space=pl.ANY)] * 2,
        out_shape=jax.ShapeDtypeStruct((ROWS, ZD, W), jnp.float32),
        scratch_shapes=[
            pltpu.VMEM(moved.shape, moved.dtype),
            pltpu.VMEM(bands.shape, bands.dtype),
            pltpu.SemaphoreType.DMA((2, steps)),
            pltpu.VMEM((2, GROUP, SPAN // 2, 16, XQ), jnp.bfloat16),
            pltpu.VMEM((4, GROUP, SPAN // 4, 16, XQ), jnp.bfloat16),
            pltpu.VMEM((ZD, TILES * 16, XQ), jnp.float32),
        ],
        compiler_params=parameters(),
        name="project",
    )(off, weights, moved, bands)


def body(tilts, tilt_defocus, defocus_table, slab_pick, interp_offset, interp_weights):
    def swap(block, bit):
        return lax.ppermute(block, "slab", [(i, i ^ bit) for i in range(4)])

    own = tilts[0]
    beside = swap(own, 1)
    across = swap(own, 2)
    entries = jnp.arange(defocus_table.shape[0], dtype=jnp.int32)
    group_defocus = jnp.sum(jnp.where(entries == slab_pick[0], defocus_table, 0.0))
    focus = tilt_defocus + group_defocus
    slab = lax.axis_index("slab").astype(jnp.int32).reshape(1)
    forward, inverse = x_tables()
    fh, fl = (jnp.asarray(t) for t in split_np(forward))
    ih, il = (jnp.asarray(t) for t in split_np(inverse))
    near, mix, gain = run_near(focus, slab, own, beside, fh, fl)
    near, across = lax.optimization_barrier((near, across))
    opposite = swap(across, 1)
    weights = interp_weights.astype(jnp.float32).reshape(TILTS, ZD * TAPS)
    bands = run_band(interp_offset, weights)
    filtered = run_main(across, opposite, near, mix, gain, fh, fl, ih, il)
    moved = lax.all_to_all(filtered, "dev", split_axis=0, concat_axis=0, tiled=True)
    return run_project(interp_offset, weights, moved, bands)


def solution(mesh):
    in_specs = (
        P("dev", "slab", None),
        P("dev"),
        P(),
        P("slab"),
        P(None, "slab"),
        P(None, "slab", None),
    )
    out_specs = P("dev", "slab", None)
    return jax.shard_map(body, mesh=mesh, in_specs=in_specs, out_specs=out_specs, check_vma=False)
```

time: 135 us -> 99.5 us (0.74)
  waiting for transfers between devices: 51.2 us -> 29.3 us
  between operations: 15.4 us -> 1.92 us
  matrix products: 3.34 us -> 0 us
  other arithmetic: 4.56 us -> 1.25 us
  starting transfers between devices: 9.86 us -> 12.7 us
  Pallas kernels: 48.8 us -> 51.6 us
    all_gather x1 -> x0, waiting for transfers between devices: 25.4 us -> none  [body(): whole = lax.all_gather(tilts, 'slab', axis=1, tiled=True)]
    ppermute x0 -> x3, waiting for transfers between devices: none -> 4.65 us  [swap(): return lax.ppermute(block, 'slab', [(i, i ^ bit) for i in range(4)])]
    dot_general x1 -> x0, matrix products: 3.34 us -> none  [responses(): mixed = jnp.dot(side, right, precision=lax.Precision.HIGHEST)]
    pallas_call x2 -> x3, Pallas kernels: 40.1 us -> 43 us  [the longest x1 22.2 us: run_main(): pl.pallas_call(main_kernel, in_specs=[pl.BlockSpec(memory_space=pl.ANY)]...]
    ppermute x0 -> x3, starting transfers between devices: none -> 1.92 us  [swap(): return lax.ppermute(block, 'slab', [(i, i ^ bit) for i in range(4)])]
    another operation x2 -> x0, other arithmetic: 1.42 us -> none  [responses(): gx = jnp.stack([jnp.cos(angle_x), jnp.sin(angle_x)], axis=1)]
  transfers between devices with their start and end apart: 2 -> 4, of which waited for: 2 -> 3; matrix products, arithmetic and copies ran while one was open for 7% -> 3% of each run, Pallas kernels for 6% -> 17%
where the time goes in v2:
time: 99.5 us; the launch traced here: 99 us
  Pallas kernels  51.6 us (52%)
  waiting for transfers between devices  29.3 us (29%)
  starting transfers between devices  12.7 us (13%)
  local copies, waits for them, and re-layouts  2.2 us (2%)
  between operations  1.92 us (2%)
  other arithmetic  1.25 us (1%)
    all_to_all x1, waiting for transfers between devices, body(): lax.all_to_all(filtered, 'dev', split_axis=0, concat_axis=0, tiled=True)  24.7 us
    pallas_call x1, Pallas kernels, run_main(): pl.pallas_call(main_kernel, in_specs=[pl.BlockSpec(memory_space=pl.ANY)]...  22.2 us
    pallas_call x1, Pallas kernels, run_project(): pl.pallas_call(project_kernel, in_specs=[scalar_spec()] * 2 + [pl.BlockSp...  12.4 us
    all_to_all x1, starting transfers between devices, body(): lax.all_to_all(filtered, 'dev', split_axis=0, concat_axis=0, tiled=True)  10.8 us
    pallas_call x1, Pallas kernels, run_band(): pl.pallas_call(band_kernel, grid=(steps,), in_specs=[pl.BlockSpec(memory_...  8.58 us
    pallas_call x1, Pallas kernels, run_near(): pl.pallas_call(near_kernel, in_specs=[scalar_spec()] * 2 + [pl.BlockSpec(...  8.43 us
    ppermute x3, waiting for transfers between devices, swap(): return lax.ppermute(block, 'slab', [(i, i ^ bit) for i in range(4)])  4.65 us
  transfers between devices with their start and end apart: 4, of which 3 were waited for; matrix products, arithmetic and copies ran while one was open for 3% of the time, Pallas kernels for 17%

profile of v2, /device:TPU:2, one launch (start us, length us, event | category | flops | bytes accessed | tf_op | source)
XLA Modules:
  0.0 99.0 jit_solution(5444129986178422848)
XLA Ops:
  0.0 0.0 collective-permute-start
  0.0 1.9 %collective-permute-start.1 = (bf16[96,3072]{1,0:T(8,128)(2,1)}, bf16[96,3072]{1,0:T(8,128)(2,1)S(1)}, u32[]{:S(2)}, u32[]{:S(2)}) collective-permute-start(bf16[96,3072]{1,0:T(8,128)(2,1)} %bitcast.8), channel_id=1, source_target_pairs={{0,64},{32,96},{64,0},{96,32},{1,65},{33,97},{65,1},{97,33},{2,66}... | collective-permute-start | bytes 1769480 | tf_op jit(solution)/shard_map/ppermute | solution.py:545
  3.2 1.3 %fusion = f32[]{:T(128)} fusion(f32[8]{0:T(128)} %param.16, s32[]{:T(128)} %bitcast.6), kind=kLoop, calls=%fused_computation.1 | loop fusion | flops 23 | bytes 40 | tf_op jit(solution)/shard_map/reduce_sum | solution.py:551
  5.0 0.0 collective-permute-done.xb_ref
  5.0 8.4 %near.1 = (f32[12,192,256]{2,1,0:T(8,128)}, bf16[2,384,768]{2,1,0:T(8,128)(2,1)}, f32[12,2,256]{2,1,0:T(2,128)}) custom-call(f32[1]{0:T(128)S(6)} %add.7.focus_ref, s32[1]{0:T(128)} %bitcast.3.slab_ref, bf16[96,3072]{1,0:T(8,128)(2,1)} %bitcast.9, bf16[96,3072]{1,0:T(8,128)(2,1)} %collective-permute-done.xb_ref, ...), custom_call_target="tpu_custom_call" | custom-call | tf_op jit(solution)/shard_map/near/pallas_call | solution.py:279
  13.5 2.7 %collective-permute-done.1.xa_any = bf16[96,3072]{1,0:T(8,128)(2,1)S(1)} collective-permute-done((bf16[96,3072]{1,0:T(8,128)(2,1)}, bf16[96,3072]{1,0:T(8,128)(2,1)S(1)}, u32[]{:S(2)}, u32[]{:S(2)}) %collective-permute-start.1) | collective-permute-done | bytes 589856 | tf_op jit(solution)/shard_map/ppermute | solution.py:545
  16.1 0.0 copy-start
  16.1 0.0 collective-permute-start.2
  16.1 2.0 %collective-permute-done.2.xb_any = bf16[96,3072]{1,0:T(8,128)(2,1)S(1)} collective-permute-done((bf16[96,3072]{1,0:T(8,128)(2,1)S(1)}, bf16[96,3072]{1,0:T(8,128)(2,1)S(1)}, u32[]{:S(2)}, u32[]{:S(2)}) %collective-permute-start.2) | collective-permute-done | bytes 589856 | tf_op jit(solution)/shard_map/ppermute | solution.py:545
  18.1 0.0 copy-start.1
  18.1 0.8 copy-done.1
  19.0 0.0 copy-done
  19.0 22.2 %main.1 = bf16[32,18,16,128]{3,2,1,0:T(8,128)(2,1)} custom-call(bf16[96,3072]{1,0:T(8,128)(2,1)} %copy-done, bf16[96,3072]{1,0:T(8,128)(2,1)} %copy-done.1, f32[12,192,256]{2,1,0:T(8,128)} %get-tuple-element.12.near_any, bf16[12,256,256]{2,1,0:T(8,128)(2,1)} %constant.24.clone.fh_ref.fh_any, bf16[12,256,256]{2,1,0:T(8,128)(2,1)} %constant.25.clone.fl_ref.fl_any, ...), custom_call_target="tpu_custom_call" | custom-call | tf_op jit(solution)/shard_map/main/pallas_call | solution.py:381
  41.1 0.0 copy-start.3
  41.1 0.0 copy-start.2
  41.2 10.8 %all-to-all-start = ((bf16[32,18,16,128]{3,2,1,0:T(8,128)(2,1)}), bf16[32,18,16,128]{3,2,1,0:T(8,128)(2,1)}, u32[]{:S(2)}, u32[]{:S(2)}) async-start(bf16[32,18,16,128]{3,2,1,0:T(8,128)(2,1)} %main.1), calls=%async_computation | async-start | bytes 4718592 | tf_op jit(solution)/shard_map/all_to_all | solution.py:563
  52.0 0.0 copy-done.3
  52.0 0.7 copy.20.off_ref
  52.7 0.0 copy-done.2
  52.7 0.7 copy.21.weight_ref
  53.4 8.6 %shard_map.136.band_any = bf16[8,4,4,256,128]{4,3,2,1,0:T(8,128)(2,1)} custom-call(s32[32,4]{1,0:T(8,128)} %copy.20.off_ref, f32[32,16]{1,0:T(8,128)} %copy.21.weight_ref), custom_call_target="tpu_custom_call" | custom-call | tf_op jit(solution)/shard_map/pallas_call | solution.py:418
  61.9 24.7 %all-to-all-done.x_any = bf16[32,18,16,128]{3,2,1,0:T(8,128)(2,1)} async-done(((bf16[32,18,16,128]{3,2,1,0:T(8,128)(2,1)}), bf16[32,18,16,128]{3,2,1,0:T(8,128)(2,1)}, u32[]{:S(2)}, u32[]{:S(2)}) %all-to-all-start) | async-done | bytes 2359328 | tf_op jit(solution)/shard_map/all_to_all | solution.py:563
  86.6 12.4 %project.1 = f32[12,4,3072]{2,1,0:T(4,128)} custom-call(s32[32,4]{1,0:T(8,128)} %copy.20.off_ref, f32[32,16]{1,0:T(8,128)} %copy.21.weight_ref, bf16[32,18,16,128]{3,2,1,0:T(8,128)(2,1)} %all-to-all-done.x_any, bf16[8,4,4,256,128]{4,3,2,1,0:T(8,128)(2,1)} %shard_map.136.band_any), custom_call_target="tpu_custom_call" | custom-call | tf_op jit(solution)/shard_map/project/pallas_call | solution.py:526
Async XLA Ops:
  0.0 5.0 %collective-permute-start = (bf16[96,3072]{1,0:T(8,128)(2,1)}, bf16[96,3072]{1,0:T(8,128)(2,1)}, u32[]{:S(2)}, u32[]{:S(2)}) collective-permute-start(bf16[96,3072]{1,0:T(8,128)(2,1)} %bitcast.7), channel_id=1, source_target_pairs={{0,32},{32,0},{64,96},{96,64},{1,33},{33,1},{65,97},{97,65},{2,34}... | collective-permute-start | bytes 1769480 | tf_op jit(solution)/shard_map/ppermute | solution.py:545
  0.0 16.1 %collective-permute-start.1 = (bf16[96,3072]{1,0:T(8,128)(2,1)}, bf16[96,3072]{1,0:T(8,128)(2,1)S(1)}, u32[]{:S(2)}, u32[]{:S(2)}) collective-permute-start(bf16[96,3072]{1,0:T(8,128)(2,1)} %bitcast.8), channel_id=1, source_target_pairs={{0,64},{32,96},{64,0},{96,32},{1,65},{33,97},{65,1},{97,33},{2,66}... | collective-permute-start | bytes 1769480 | tf_op jit(solution)/shard_map/ppermute | solution.py:545
  16.1 2.8 %copy-start = (bf16[96,3072]{1,0:T(8,128)(2,1)}, bf16[96,3072]{1,0:T(8,128)(2,1)S(1)}, u32[]{:S(2)}) copy-start(bf16[96,3072]{1,0:T(8,128)(2,1)S(1)} %collective-permute-done.1.xa_any) | copy-start | bytes 1769476
  16.1 2.0 %collective-permute-start.2 = (bf16[96,3072]{1,0:T(8,128)(2,1)S(1)}, bf16[96,3072]{1,0:T(8,128)(2,1)S(1)}, u32[]{:S(2)}, u32[]{:S(2)}) collective-permute-start(bf16[96,3072]{1,0:T(8,128)(2,1)S(1)} %collective-permute-done.1.xa_any), channel_id=1, source_target_pairs={{0,32},{32,0},{64,96},{96,64},{1,33},{33,1},{65,97},{97,65},{2,34}... | collective-permute-start | bytes 1769480 | tf_op jit(solution)/shard_map/ppermute | solution.py:545
  18.1 0.8 copy-start.1
  41.1 10.8 %copy-start.3 = (s32[32,4]{0,1:T(4,128)S(1)}, s32[32,4]{0,1:T(4,128)}, u32[]{:S(2)}) copy-start(s32[32,4]{0,1:T(4,128)} %param.18) | copy-start | bytes 1540
  41.1 11.5 %copy-start.2 = (bf16[32,4,4]{0,2,1:T(4,128)(2,1)S(1)}, bf16[32,4,4]{0,2,1:T(4,128)(2,1)}, u32[]{:S(2)}) copy-start(bf16[32,4,4]{0,2,1:T(4,128)(2,1)} %param.19) | copy-start | bytes 3076
  41.2 45.5 %all-to-all-start = ((bf16[32,18,16,128]{3,2,1,0:T(8,128)(2,1)}), bf16[32,18,16,128]{3,2,1,0:T(8,128)(2,1)}, u32[]{:S(2)}, u32[]{:S(2)}) async-start(bf16[32,18,16,128]{3,2,1,0:T(8,128)(2,1)} %main.1), calls=%async_computation | async-start | bytes 4718592 | tf_op jit(solution)/shard_map/all_to_all | solution.py:563

commit v3 on v2

--- a/solution.py
+++ b/solution.py
@@ -204,8 +204,8 @@
 STRIP = 16
 
 
-def load_strips(x_refs, vh, vl):
-    for n, x_ref in enumerate(x_refs):
+def load_strips(x_refs, vh, vl, place=0):
+    for n, x_ref in enumerate(x_refs, place):
 
         def strip(i, carry):
             rows = pl.ds(pl.multiple_of(i * STRIP, STRIP), STRIP)
@@ -228,15 +228,11 @@
         lax.fori_loop(0, QUARTER // STRIP, strip, 0)
 
 
-def near_kernel(focus_ref, slab_ref, xa_ref, xb_ref, fh_ref, fl_ref, left_ref, right_ref, fy_ref,
-                fx_ref, out_ref, mix_ref, gain_ref, vh, vl):
+def near_kernel(focus_ref, slab_ref, xa_ref, xb_ref, fh, fl, left_ref, right_ref, fy_ref, fx_ref,
+                out_ref, mix_ref, gain_ref, vh, vl):
     load_strips((xa_ref, xb_ref), vh, vl)
-
-    def column(j, carry):
-        out_ref[j] = three_products(vh[j], vl[j], fh_ref[j], fl_ref[j])
-        return carry
-
-    lax.fori_loop(0, NJ, column, 0)
+    for j in range(NJ):
+        out_ref[j] = three_products(vh[j], vl[j], fh[j], fl[j])
     scale = chi_scale * focus_ref[0]
     slab = slab_ref[0]
     angle_x = scale * (fx_ref[...] * fx_ref[...])
@@ -259,16 +255,16 @@
         mix_ref[odd] = jnp.concatenate([high, low, high], axis=1)
 
 
-def parameters():
-    return pltpu.CompilerParams(vmem_limit_bytes=63 * 2**20)
+def parameters(megabytes):
+    return pltpu.CompilerParams(vmem_limit_bytes=megabytes * 2**20)
 
 
 def scalar_spec():
     return pl.BlockSpec(memory_space=pltpu.SMEM)
 
 
-def halves():
-    return [pltpu.VMEM((NJ, HALF, 2 * XQ), jnp.bfloat16)] * 2
+def vmem_spec():
+    return pl.BlockSpec(memory_space=pltpu.VMEM)
 
 
 def run_near(focus, slab, xa, xb, fh, fl):
@@ -278,75 +274,45 @@
     fx = x_frequencies().astype(np.float32)
     return pl.pallas_call(
         near_kernel,
-        in_specs=[scalar_spec()] * 2 + [pl.BlockSpec(memory_space=pltpu.VMEM)] * 8,
+        in_specs=[scalar_spec()] * 2 + [vmem_spec()] * 8,
+        out_specs=[vmem_spec()] * 3,
         out_shape=[
             jax.ShapeDtypeStruct((NJ, HALF, 2 * XQ), jnp.float32),
             jax.ShapeDtypeStruct((2, YB, 3 * DEPTH), jnp.bfloat16),
             jax.ShapeDtypeStruct((NJ, 2, 2 * XQ), jnp.float32),
         ],
-        scratch_shapes=halves(),
-        compiler_params=parameters(),
+        scratch_shapes=[pltpu.VMEM((NJ, HALF, 2 * XQ), jnp.bfloat16)] * 2,
+        compiler_params=parameters(NEAR_MB),
         name="near",
     )(focus, slab, xa, xb, fh, fl, *(jnp.asarray(t) for t in (left, right, fy, fx)))
 
 
-def main_kernel(xa_any, xb_any, near_any, fh_any, fl_any, mix_any, gain_any, ih_any, il_any,
-                out_any, xa, xb, near, fh, fl, mix, gain, ih, il, vh, vl, back, out,
-                early, late, sent):
-    first = [(xa_any, xa), (xb_any, xb), (mix_any, mix), (gain_any, gain)]
-    copies = [pltpu.make_async_copy(a, b, early.at[i]) for i, (a, b) in enumerate(first)]
-    for copy in copies[:2]:
-        copy.start()
-    streams = [(near_any, near), (fh_any, fh), (fl_any, fl), (ih_any, ih), (il_any, il)]
-
-    def stream(n, j):
-        source, target = streams[n]
-        return pltpu.make_async_copy(source.at[j], target.at[j], late.at[n, j])
-
-    for j in range(NJ):
-        for n in range(len(streams)):
-            stream(n, j).start()
-        if j == 0:
-            for copy in copies[2:]:
-                copy.start()
-    for copy in copies[:2]:
-        copy.wait()
+NEAR_MB = 24
+MAIN_MB = 40
+BAND_MB = 16
+PROJECT_MB = 24
+
+
+def main_kernel(xa, xb, near, mix, gain, fh, fl, ih, il, out, vh, vl, eh, el, oh, ol, zh, zl, back):
     load_strips((xa, xb), vh, vl)
-    for copy in copies[2:]:
-        copy.wait()
-    empty = jnp.zeros((DEPTH - HALF, 2 * XQ), jnp.bfloat16)
-
-    def column(j, carry):
-        for n in range(len(streams)):
-            stream(n, j).wait()
+    for j in range(NJ):
         far = three_products(vh[j], vl[j], fh[j], fl[j])
         here = near[j]
+        eh[j], el[j] = split(here + far)
+        oh[j], ol[j] = split(here - far)
+    empty = jnp.zeros((DEPTH - HALF, 2 * XQ), jnp.bfloat16)
+    for j in range(NJ):
         factors = gain[j]
 
-        def mixed(odd, value):
-            high, low = split(value)
+        def mixed(odd, high, low):
             right = jnp.concatenate([high, empty, high, empty, low, empty], axis=0)
             y = jnp.dot(mix[odd], right, preferred_element_type=jnp.float32)
             return y[:HALF] * factors[0:1] + y[HALF:] * factors[1:2]
 
-        even = mixed(0, here + far)
-        odd = mixed(1, here - far)
-        high, low = split(jnp.concatenate([even + odd, even - odd], axis=0))
-        back[j] = three_products(high, low, ih[j], il[j])
-        return carry
-
-    lax.fori_loop(0, NJ, column, 0)
-
-    def blocks_of(start):
-        cut = pl.ds(pl.multiple_of(start, 8), 8)
-        v = {}
-        for jj in range(NJ):
-            one, two = back[jj, cut, 0:XQ], back[jj, cut, XQ : 2 * XQ]
-            if jj == 0:
-                v[0], v[12] = (one, None), (two, None)
-            else:
-                v[jj] = (one, two)
-        return inverse_24(v)
+        even, odd = mixed(0, eh[j], el[j]), mixed(1, oh[j], ol[j])
+        zh[j], zl[j] = split(jnp.concatenate([even + odd, even - odd], axis=0))
+    for j in range(NJ):
+        back[j] = three_products(zh[j], zl[j], ih[j], il[j])
 
     devices = TILTS // 2
     for half in range(2):
@@ -355,93 +321,76 @@
             per_strip, per_tile = 8 // count, 16 // count
 
             def strip(i, carry):
-                values = blocks_of(low_row + i * 8)
+                cut = pl.ds(pl.multiple_of(low_row + i * 8, 8), 8)
+                v = {}
+                for jj in range(NJ):
+                    one, two = back[jj, cut, 0:XQ], back[jj, cut, XQ : 2 * XQ]
+                    if jj == 0:
+                        v[0], v[12] = (one, None), (two, None)
+                    else:
+                        v[jj] = (one, two)
+                values = inverse_24(v)
                 for part in range(per_strip):
-                    cut = slice(part * count, (part + 1) * count)
+                    some = slice(part * count, (part + 1) * count)
+                    place = half * devices + i * per_strip + part
                     for tile in range(XP // per_tile):
-                        pieces = [values[per_tile * tile + n][cut] for n in range(per_tile)]
-                        joined = jnp.concatenate(pieces, axis=0)
-                        place = half * devices + i * per_strip + part
+                        joined = jnp.concatenate(
+                            [values[per_tile * tile + n][some] for n in range(per_tile)], axis=0
+                        )
                         out[place, low_tile + tile] = joined.astype(jnp.bfloat16)
                 return carry
 
             lax.fori_loop(0, devices // per_strip, strip, 0)
             low_row += devices * count
             low_tile += XP // per_tile
-        cut = pl.ds(half * devices, devices)
-        pltpu.make_async_copy(out.at[cut], out_any.at[cut], sent.at[half]).start()
-    for half in range(2):
-        cut = pl.ds(half * devices, devices)
-        pltpu.make_async_copy(out.at[cut], out_any.at[cut], sent.at[half]).wait()
 
 
 def run_main(xa, xb, near, mix, gain, fh, fl, ih, il):
-    shape = (TILTS, TILES, 16, XQ)
-    args = (xa, xb, near, fh, fl, mix, gain, ih, il)
+    args = (xa, xb, near, mix, gain, fh, fl, ih, il)
+    half = pltpu.VMEM((NJ, HALF, 2 * XQ), jnp.bfloat16)
+    full = pltpu.VMEM((NJ, YB, 2 * XQ), jnp.bfloat16)
     return pl.pallas_call(
         main_kernel,
-        in_specs=[pl.BlockSpec(memory_space=pl.ANY)] * len(args),
-        out_specs=pl.BlockSpec(memory_space=pl.ANY),
-        out_shape=jax.ShapeDtypeStruct(shape, jnp.bfloat16),
-        scratch_shapes=[pltpu.VMEM(a.shape, a.dtype) for a in args]
-        + halves()
-        + [
-            pltpu.VMEM((NJ, YB, 2 * XQ), jnp.float32),
-            pltpu.VMEM(shape, jnp.bfloat16),
-            pltpu.SemaphoreType.DMA((4,)),
-            pltpu.SemaphoreType.DMA((5, NJ)),
-            pltpu.SemaphoreType.DMA((2,)),
-        ],
-        compiler_params=parameters(),
+        in_specs=[vmem_spec()] * len(args),
+        out_specs=vmem_spec(),
+        out_shape=jax.ShapeDtypeStruct((TILTS, TILES, 16, XQ), jnp.bfloat16),
+        scratch_shapes=[half] * 6 + [full] * 2 + [pltpu.VMEM((NJ, YB, 2 * XQ), jnp.float32)],
+        compiler_params=parameters(MAIN_MB),
         name="main",
     )(*args)
 
 
 def band_kernel(off_ref, weight_ref, out_ref):
-    step = pl.program_id(0)
     distance = lax.broadcasted_iota(jnp.int32, (2 * XQ, XQ), 0) - lax.broadcasted_iota(
         jnp.int32, (2 * XQ, XQ), 1
     )
-    for z in range(ZD):
-        for g in range(GROUP):
-            t = step * GROUP + g
+    distance = distance.astype(jnp.int16)
+
+    def tilt(t, carry):
+        for z in range(ZD):
             shift = off_ref[t, z] & (XQ - 1)
-            moved = distance - shift
-            band = jnp.zeros((2 * XQ, XQ), jnp.float32)
+            band = jnp.zeros((2 * XQ, XQ), jnp.bfloat16)
             for tap in range(TAPS):
-                band = jnp.where(moved == tap, weight_ref[t, z * TAPS + tap], band)
-            out_ref[0, z, g] = band.astype(jnp.bfloat16)
+                weight = weight_ref[t, z * TAPS + tap].astype(jnp.bfloat16)
+                band = jnp.where(distance == (shift + tap).astype(jnp.int16), weight, band)
+            out_ref[t // GROUP, z, t % GROUP] = band
+        return carry
+
+    lax.fori_loop(0, TILTS, tilt, 0)
 
 
 def run_band(off, weights):
-    steps = TILTS // GROUP
     return pl.pallas_call(
         band_kernel,
-        grid=(steps,),
-        in_specs=[
-            pl.BlockSpec(memory_space=pltpu.SMEM),
-            pl.BlockSpec(memory_space=pltpu.SMEM),
-        ],
-        out_specs=pl.BlockSpec((1, ZD, GROUP, 2 * XQ, XQ), lambda i: (i, 0, 0, 0, 0)),
-        out_shape=jax.ShapeDtypeStruct((steps, ZD, GROUP, 2 * XQ, XQ), jnp.bfloat16),
-        compiler_params=pltpu.CompilerParams(dimension_semantics=("arbitrary",)),
+        in_specs=[scalar_spec()] * 2,
+        out_specs=vmem_spec(),
+        out_shape=jax.ShapeDtypeStruct((TILTS // GROUP, ZD, GROUP, 2 * XQ, XQ), jnp.bfloat16),
+        compiler_params=parameters(BAND_MB),
+        name="bands",
     )(off, weights)
 
 
-def project_kernel(off_ref, weight_ref, x_any, band_any, out_ref, x, bands, arrived, wide, narrow,
-                   total):
-    steps = TILTS // GROUP
-
-    def fetch(i):
-        some = pl.ds(i * GROUP, GROUP)
-        return (
-            pltpu.make_async_copy(x_any.at[some], x.at[some], arrived.at[0, i]),
-            pltpu.make_async_copy(band_any.at[i], bands.at[i], arrived.at[1, i]),
-        )
-
-    for i in range(steps):
-        for copy in fetch(i):
-            copy.start()
+def project_kernel(off_ref, weight_ref, x, bands, out_ref, wide, narrow, total):
     wide[...] = jnp.zeros_like(wide)
     narrow[...] = jnp.zeros_like(narrow)
     total[...] = jnp.zeros_like(total)
@@ -461,10 +410,11 @@
         return jnp.concatenate(pieces, axis=0)
 
     def step(i, carry):
-        for copy in fetch(i):
-            copy.wait()
+        late = 0
         for g in range(GROUP):
             t = i * GROUP + g
+            for z in range(ZD):
+                late += jnp.where((off_ref[t, z] & (XQ - 1)) > XQ - TAPS + 1, 1, 0)
             for padded, count, per_tile, tiles, base in layouts:
                 lead = LEFT // per_tile
                 rows = [x[t, base + p].astype(jnp.float32) for p in range(tiles)]
@@ -487,9 +437,11 @@
             band = bands[i, z].reshape(GROUP * 2 * XQ, XQ)
             total[z] += jnp.dot(left, band, preferred_element_type=jnp.float32)
 
-        for g in range(GROUP):
-            t = i * GROUP + g
-            for z in range(ZD):
+        @pl.when(late > 0)
+        def _():
+            def pair(n, carry):
+                g, z = n // ZD, n % ZD
+                t = i * GROUP + g
                 shift = off_ref[t, z] & (XQ - 1)
 
                 @pl.when(shift > XQ - TAPS + 1)
@@ -509,9 +461,13 @@
                         preferred_element_type=jnp.float32,
                     )
 
+                return carry
+
+            lax.fori_loop(0, GROUP * ZD, pair, 0)
+
         return carry
 
-    lax.fori_loop(0, steps, step, 0)
+    lax.fori_loop(0, TILTS // GROUP, step, 0)
     for z in range(ZD):
         for (first, count), (_, _, _, _, base) in zip(PARTS, layouts):
             for b in range(XP):
@@ -522,20 +478,17 @@
 
 
 def run_project(off, weights, moved, bands):
-    steps = TILTS // GROUP
     return pl.pallas_call(
         project_kernel,
-        in_specs=[scalar_spec()] * 2 + [pl.BlockSpec(memory_space=pl.ANY)] * 2,
+        in_specs=[scalar_spec()] * 2 + [vmem_spec()] * 2,
+        out_specs=vmem_spec(),
         out_shape=jax.ShapeDtypeStruct((ROWS, ZD, W), jnp.float32),
         scratch_shapes=[
-            pltpu.VMEM(moved.shape, moved.dtype),
-            pltpu.VMEM(bands.shape, bands.dtype),
-            pltpu.SemaphoreType.DMA((2, steps)),
             pltpu.VMEM((2, GROUP, SPAN // 2, 16, XQ), jnp.bfloat16),
             pltpu.VMEM((4, GROUP, SPAN // 4, 16, XQ), jnp.bfloat16),
             pltpu.VMEM((ZD, TILES * 16, XQ), jnp.float32),
         ],
-        compiler_params=parameters(),
+        compiler_params=parameters(PROJECT_MB),
         name="project",
     )(off, weights, moved, bands)
 

time: 99.5 us -> 90.2 us (0.907)
  Pallas kernels: 51.6 us -> 28.6 us
  local copies, waits for them, and re-layouts: 2.2 us -> 15.6 us
    pallas_call x4, Pallas kernels: 51.6 us -> 28.6 us  [the longest x1 10.9 us: run_main(): pl.pallas_call(main_kernel, in_specs=[vmem_spec()] * len(args), out_specs...]
    unnamed x9 -> x31, local copies, waits for them, and re-layouts: 1.51 us -> 15.5 us
    ppermute x3, waiting for transfers between devices: 4.65 us -> 2.5 us  [swap(): return lax.ppermute(block, 'slab', [(i, i ^ bit) for i in range(4)])]
    all_to_all x1, waiting for transfers between devices: 24.7 us -> 26.8 us  [body(): lax.all_to_all(filtered, 'dev', split_axis=0, concat_axis=0, tiled=True)]
  transfers between devices with their start and end apart: 4 -> 4, of which waited for: 3 -> 3; matrix products, arithmetic and copies ran while one was open for 3% -> 2% of each run, Pallas kernels for 17% -> 8%
where the time goes in v3:
time: 90.2 us; the launch traced here: 89.7 us
  waiting for transfers between devices  29.3 us (32%)
  Pallas kernels  28.6 us (32%)
  local copies, waits for them, and re-layouts  15.6 us (17%)
  starting transfers between devices  12.8 us (14%)
  between operations  2.08 us (2%)
  other arithmetic  1.34 us (1%)
    all_to_all x1, waiting for transfers between devices, body(): lax.all_to_all(filtered, 'dev', split_axis=0, concat_axis=0, tiled=True)  26.8 us
    unnamed x31, local copies, waits for them, and re-layouts  15.5 us
    all_to_all x1, starting transfers between devices, body(): lax.all_to_all(filtered, 'dev', split_axis=0, concat_axis=0, tiled=True)  10.9 us
    pallas_call x1, Pallas kernels, run_main(): pl.pallas_call(main_kernel, in_specs=[vmem_spec()] * len(args), out_specs...  10.9 us
    pallas_call x1, Pallas kernels, run_project(): pl.pallas_call(project_kernel, in_specs=[scalar_spec()] * 2 + [vmem_spec(...  10.4 us
    pallas_call x1, Pallas kernels, run_band(): pl.pallas_call(band_kernel, in_specs=[scalar_spec()] * 2, out_specs=vmem_...  4.35 us
    pallas_call x1, Pallas kernels, run_near(): pl.pallas_call(near_kernel, in_specs=[scalar_spec()] * 2 + [vmem_spec()]...  2.94 us
    ppermute x3, waiting for transfers between devices, swap(): return lax.ppermute(block, 'slab', [(i, i ^ bit) for i in range(4)])  2.5 us
  transfers between devices with their start and end apart: 4, of which 3 were waited for; matrix products, arithmetic and copies ran while one was open for 2% of the time, Pallas kernels for 8%

profile of v3, /device:TPU:2, one launch (start us, length us, event | category | flops | bytes accessed | tf_op | source)
XLA Modules:
  0.0 89.7 jit_solution(7441091474280702184)
XLA Ops:
  0.0 1.9 %collective-permute-start.1 = (bf16[96,3072]{1,0:T(8,128)(2,1)}, bf16[96,3072]{1,0:T(8,128)(2,1)S(1)}, u32[]{:S(2)}, u32[]{:S(2)}) collective-permute-start(bf16[96,3072]{1,0:T(8,128)(2,1)} %bitcast.8), channel_id=1, source_target_pairs={{0,64},{32,96},{64,0},{96,32},{1,65},{33,97},{65,1},{97,33},{2,66}... | collective-permute-start | bytes 1769480 | tf_op jit(solution)/shard_map/ppermute | solution.py:498
  3.2 1.3 %fusion = f32[]{:T(128)} fusion(f32[8]{0:T(128)} %param.16, s32[]{:T(128)} %bitcast.6), kind=kLoop, calls=%fused_computation.1 | loop fusion | flops 23 | bytes 40 | tf_op jit(solution)/shard_map/reduce_sum | solution.py:504
  5.3 0.0 copy-start.2
  5.3 1.4 %copy-done.2 = bf16[12,256,256]{2,1,0:T(8,128)(2,1)S(1)} copy-done((bf16[12,256,256]{2,1,0:T(8,128)(2,1)S(1)}, bf16[12,256,256]{2,1,0:T(8,128)(2,1)}, u32[]{:S(2)}) %copy-start.2) | copy-done | bytes 1572888
  6.7 1.4 %copy-done.4 = bf16[12,256,256]{2,1,0:T(8,128)(2,1)S(1)} copy-done((bf16[12,256,256]{2,1,0:T(8,128)(2,1)S(1)}, bf16[12,256,256]{2,1,0:T(8,128)(2,1)}, u32[]{:S(2)}) %copy-start.4) | copy-done | bytes 1572888
  8.1 1.1 %copy-done.8 = f32[2,2,192,192]{3,2,1,0:T(8,128)S(1)} copy-done((f32[2,2,192,192]{3,2,1,0:T(8,128)S(1)}, f32[2,2,192,192]{3,2,1,0:T(8,128)}, u32[]{:S(2)}) %copy-start.8) | copy-done | bytes 589848
  9.2 1.1 %copy-done.9 = bf16[1,96,3072]{2,1,0:T(8,128)(2,1)S(1)} copy-done((bf16[1,96,3072]{2,1,0:T(8,128)(2,1)S(1)}, bf16[1,96,3072]{2,1,0:T(8,128)(2,1)}, u32[]{:S(2)}) %copy-start.9) | copy-done | bytes 589848
  10.3 1.0 %copy-done.10 = f32[2,192,192]{2,1,0:T(8,128)S(1)} copy-done((f32[2,192,192]{2,1,0:T(8,128)S(1)}, f32[2,192,192]{2,1,0:T(8,128)}, u32[]{:S(2)}) %copy-start.10) | copy-done | bytes 294936
  11.3 0.7 copy-done.11
  12.0 0.7 copy-done.12
  12.7 2.9 %near.1 = (f32[12,192,256]{2,1,0:T(8,128)S(1)}, bf16[2,384,768]{2,1,0:T(8,128)(2,1)S(1)}, f32[12,2,256]{2,1,0:T(2,128)S(1)}) custom-call(f32[1]{0:T(128)S(6)} %add.7.focus_ref, s32[1]{0:T(128)} %bitcast.3.slab_ref, bf16[96,3072]{1,0:T(8,128)(2,1)S(1)} %bitcast.9, bf16[96,3072]{1,0:T(8,128)(2,1)S(1)} %collective-permute-done.xb_ref, ...), custom_call_target="tpu_custom_call" | custom-call | tf_op jit(solution)/shard_map/near/pallas_call | solution.py:275
  15.6 0.5 collective-permute-done.1.xa
  16.1 2.0 %collective-permute-done.2.xb = bf16[96,3072]{1,0:T(8,128)(2,1)S(1)} collective-permute-done((bf16[96,3072]{1,0:T(8,128)(2,1)S(1)}, bf16[96,3072]{1,0:T(8,128)(2,1)S(1)}, u32[]{:S(2)}, u32[]{:S(2)}) %collective-permute-start.2) | collective-permute-done | bytes 589856 | tf_op jit(solution)/shard_map/ppermute | solution.py:498
  18.1 0.0 copy-start.7
  18.2 1.4 %copy-done.7 = bf16[12,256,256]{2,1,0:T(8,128)(2,1)S(1)} copy-done((bf16[12,256,256]{2,1,0:T(8,128)(2,1)S(1)}, bf16[12,256,256]{2,1,0:T(8,128)(2,1)}, u32[]{:S(2)}) %copy-start.7) | copy-done | bytes 1572888
  19.6 10.9 %main.1 = bf16[32,18,16,128]{3,2,1,0:T(8,128)(2,1)} custom-call(bf16[96,3072]{1,0:T(8,128)(2,1)S(1)} %collective-permute-done.1.xa, bf16[96,3072]{1,0:T(8,128)(2,1)S(1)} %collective-permute-done.2.xb, f32[12,192,256]{2,1,0:T(8,128)S(1)} %get-tuple-element.12.near, bf16[2,384,768]{2,1,0:T(8,128)(2,1)S(1)} %get-tuple-element.13.mix, ...), custom_call_target="tpu_custom_call" | custom-call | tf_op jit(solution)/shard_map/main/pallas_call | solution.py:352
  30.4 10.9 %all-to-all-start = ((bf16[32,18,16,128]{3,2,1,0:T(8,128)(2,1)}), bf16[32,18,16,128]{3,2,1,0:T(8,128)(2,1)S(1)}, u32[]{:S(2)}, u32[]{:S(2)}) async-start(bf16[32,18,16,128]{3,2,1,0:T(8,128)(2,1)} %main.1), calls=%async_computation | async-start | bytes 4718592 | tf_op jit(solution)/shard_map/all_to_all | solution.py:516
  41.3 0.1 copy.20.off_ref
  41.4 0.1 copy.21.weight_ref
  41.5 4.3 %bands.1 = bf16[8,4,4,256,128]{4,3,2,1,0:T(8,128)(2,1)S(1)} custom-call(s32[32,4]{1,0:T(8,128)S(1)} %copy.20.off_ref, f32[32,16]{1,0:T(8,128)S(1)} %copy.21.weight_ref), custom_call_target="tpu_custom_call" | custom-call | tf_op jit(solution)/shard_map/bands/pallas_call | solution.py:383
  45.9 3.2 %copy-done = bf16[8,4,4,256,128]{4,3,2,1,0:T(8,128)(2,1)} copy-done((bf16[8,4,4,256,128]{4,3,2,1,0:T(8,128)(2,1)}, bf16[8,4,4,256,128]{4,3,2,1,0:T(8,128)(2,1)S(1)}, u32[]{:S(2)}) %copy-start) | copy-done | bytes 8388632
  49.1 26.8 %all-to-all-done.x = bf16[32,18,16,128]{3,2,1,0:T(8,128)(2,1)S(1)} async-done(((bf16[32,18,16,128]{3,2,1,0:T(8,128)(2,1)}), bf16[32,18,16,128]{3,2,1,0:T(8,128)(2,1)S(1)}, u32[]{:S(2)}, u32[]{:S(2)}) %all-to-all-start) | async-done | bytes 2359328 | tf_op jit(solution)/shard_map/all_to_all | solution.py:516
  75.9 3.4 %copy-done.1 = bf16[8,4,4,256,128]{4,3,2,1,0:T(8,128)(2,1)S(1)} copy-done((bf16[8,4,4,256,128]{4,3,2,1,0:T(8,128)(2,1)S(1)}, bf16[8,4,4,256,128]{4,3,2,1,0:T(8,128)(2,1)}, u32[]{:S(2)}) %copy-start.1) | copy-done | bytes 8388632
  79.3 10.4 %project.1 = f32[12,4,3072]{2,1,0:T(4,128)} custom-call(s32[32,4]{1,0:T(8,128)S(1)} %copy.20.off_ref, f32[32,16]{1,0:T(8,128)S(1)} %copy.21.weight_ref, bf16[32,18,16,128]{3,2,1,0:T(8,128)(2,1)S(1)} %all-to-all-done.x, bf16[8,4,4,256,128]{4,3,2,1,0:T(8,128)(2,1)S(1)} %copy-done.1), custom_call_target="tpu_custom_call" | custom-call | tf_op jit(solution)/shard_map/project/pallas_call | solution.py:481
  (21 shorter events, 0.0 us)
Async XLA Ops:
  0.0 5.3 %collective-permute-start = (bf16[96,3072]{1,0:T(8,128)(2,1)}, bf16[96,3072]{1,0:T(8,128)(2,1)S(1)}, u32[]{:S(2)}, u32[]{:S(2)}) collective-permute-start(bf16[96,3072]{1,0:T(8,128)(2,1)} %bitcast.7), channel_id=1, source_target_pairs={{0,32},{32,0},{64,96},{96,64},{1,33},{33,1},{65,97},{97,65},{2,34}... | collective-permute-start | bytes 1769480 | tf_op jit(solution)/shard_map/ppermute | solution.py:498
  0.0 16.1 %collective-permute-start.1 = (bf16[96,3072]{1,0:T(8,128)(2,1)}, bf16[96,3072]{1,0:T(8,128)(2,1)S(1)}, u32[]{:S(2)}, u32[]{:S(2)}) collective-permute-start(bf16[96,3072]{1,0:T(8,128)(2,1)} %bitcast.8), channel_id=1, source_target_pairs={{0,64},{32,96},{64,0},{96,32},{1,65},{33,97},{65,1},{97,33},{2,66}... | collective-permute-start | bytes 1769480 | tf_op jit(solution)/shard_map/ppermute | solution.py:498
  5.3 1.4 %copy-start.2 = (bf16[12,256,256]{2,1,0:T(8,128)(2,1)S(1)}, bf16[12,256,256]{2,1,0:T(8,128)(2,1)}, u32[]{:S(2)}) copy-start(bf16[12,256,256]{2,1,0:T(8,128)(2,1)} %constant.25.clone.fl) | copy-start | bytes 4718596
  6.7 1.4 %copy-start.4 = (bf16[12,256,256]{2,1,0:T(8,128)(2,1)S(1)}, bf16[12,256,256]{2,1,0:T(8,128)(2,1)}, u32[]{:S(2)}) copy-start(bf16[12,256,256]{2,1,0:T(8,128)(2,1)} %constant.24.clone.fh) | copy-start | bytes 4718596
  8.1 1.1 %copy-start.8 = (f32[2,2,192,192]{3,2,1,0:T(8,128)S(1)}, f32[2,2,192,192]{3,2,1,0:T(8,128)}, u32[]{:S(2)}) copy-start(f32[2,2,192,192]{3,2,1,0:T(8,128)} %constant.29.clone.right_ref) | copy-start | bytes 1769476
  9.2 1.1 %copy-start.9 = (bf16[1,96,3072]{2,1,0:T(8,128)(2,1)S(1)}, bf16[1,96,3072]{2,1,0:T(8,128)(2,1)}, u32[]{:S(2)}) copy-start(bf16[1,96,3072]{2,1,0:T(8,128)(2,1)} %param.14) | copy-start | bytes 1769476
  10.3 1.0 %copy-start.10 = (f32[2,192,192]{2,1,0:T(8,128)S(1)}, f32[2,192,192]{2,1,0:T(8,128)}, u32[]{:S(2)}) copy-start(f32[2,192,192]{2,1,0:T(8,128)} %constant.28.clone.left_ref) | copy-start | bytes 884740
  11.3 0.7 copy-start.11
  12.0 0.7 copy-start.12
  12.7 5.5 %copy-start.3 = (bf16[12,256,256]{2,1,0:T(8,128)(2,1)S(1)}, bf16[12,256,256]{2,1,0:T(8,128)(2,1)}, u32[]{:S(2)}) copy-start(bf16[12,256,256]{2,1,0:T(8,128)(2,1)} %constant.25.clone.fl) | copy-start | bytes 4718596
  12.7 5.5 %copy-start.5 = (bf16[12,256,256]{2,1,0:T(8,128)(2,1)S(1)}, bf16[12,256,256]{2,1,0:T(8,128)(2,1)}, u32[]{:S(2)}) copy-start(bf16[12,256,256]{2,1,0:T(8,128)(2,1)} %constant.24.clone.fh) | copy-start | bytes 4718596
  12.7 5.5 %copy-start.6 = (bf16[12,256,256]{2,1,0:T(8,128)(2,1)S(1)}, bf16[12,256,256]{2,1,0:T(8,128)(2,1)}, u32[]{:S(2)}) copy-start(bf16[12,256,256]{2,1,0:T(8,128)(2,1)} %constant.27.clone.il) | copy-start | bytes 4718596
  16.1 2.0 %collective-permute-start.2 = (bf16[96,3072]{1,0:T(8,128)(2,1)S(1)}, bf16[96,3072]{1,0:T(8,128)(2,1)S(1)}, u32[]{:S(2)}, u32[]{:S(2)}) collective-permute-start(bf16[96,3072]{1,0:T(8,128)(2,1)S(1)} %collective-permute-done.1.xa), channel_id=1, source_target_pairs={{0,32},{32,0},{64,96},{96,64},{1,33},{33,1},{65,97},{97,65},{2,34}... | collective-permute-start | bytes 1769480 | tf_op jit(solution)/shard_map/ppermute | solution.py:498
  18.1 1.4 %copy-start.7 = (bf16[12,256,256]{2,1,0:T(8,128)(2,1)S(1)}, bf16[12,256,256]{2,1,0:T(8,128)(2,1)}, u32[]{:S(2)}) copy-start(bf16[12,256,256]{2,1,0:T(8,128)(2,1)} %constant.26.clone.ih) | copy-start | bytes 4718596
  30.4 10.9 %copy-start.14 = (s32[32,4]{0,1:T(4,128)S(1)}, s32[32,4]{0,1:T(4,128)}, u32[]{:S(2)}) copy-start(s32[32,4]{0,1:T(4,128)} %param.18) | copy-start | bytes 1540
  30.4 11.0 %copy-start.13 = (bf16[32,4,4]{0,2,1:T(4,128)(2,1)S(1)}, bf16[32,4,4]{0,2,1:T(4,128)(2,1)}, u32[]{:S(2)}) copy-start(bf16[32,4,4]{0,2,1:T(4,128)(2,1)} %param.19) | copy-start | bytes 3076
  30.4 45.5 %all-to-all-start = ((bf16[32,18,16,128]{3,2,1,0:T(8,128)(2,1)}), bf16[32,18,16,128]{3,2,1,0:T(8,128)(2,1)S(1)}, u32[]{:S(2)}, u32[]{:S(2)}) async-start(bf16[32,18,16,128]{3,2,1,0:T(8,128)(2,1)} %main.1), calls=%async_computation | async-start | bytes 4718592 | tf_op jit(solution)/shard_map/all_to_all | solution.py:516
  45.9 3.2 %copy-start = (bf16[8,4,4,256,128]{4,3,2,1,0:T(8,128)(2,1)}, bf16[8,4,4,256,128]{4,3,2,1,0:T(8,128)(2,1)S(1)}, u32[]{:S(2)}) copy-start(bf16[8,4,4,256,128]{4,3,2,1,0:T(8,128)(2,1)S(1)} %bands.1) | copy-start | bytes 25165828
  75.9 3.4 %copy-start.1 = (bf16[8,4,4,256,128]{4,3,2,1,0:T(8,128)(2,1)S(1)}, bf16[8,4,4,256,128]{4,3,2,1,0:T(8,128)(2,1)}, u32[]{:S(2)}) copy-start(bf16[8,4,4,256,128]{4,3,2,1,0:T(8,128)(2,1)} %copy-done) | copy-start | bytes 25165828

commit v4 on v3

--- a/solution.py
+++ b/solution.py
@@ -39,25 +39,21 @@
     return high, low
 
 
-def x_tables():
+def x_table():
     n2 = np.arange(XQ)
     k2 = np.arange(XQ)
-    forward = np.zeros((NJ, 2 * XQ, 2 * XQ))
-    inverse = np.zeros((NJ, 2 * XQ, 2 * XQ))
+    table = np.zeros((NJ, 2 * XQ, 2 * XQ))
     for j in range(NJ):
         if j == 0:
             for half, k1 in enumerate((0, 12)):
                 angle = 2 * np.pi * ((n2[:, None] * (k1 + XP * k2[None, :])) % W) / W
-                cas = np.cos(angle) + np.sin(angle)
                 cut = slice(half * XQ, (half + 1) * XQ)
-                forward[j, cut, cut] = cas
-                inverse[j, cut, cut] = cas.T / W
+                table[j, cut, cut] = np.cos(angle) + np.sin(angle)
         else:
             angle = 2 * np.pi * ((n2[:, None] * (j + XP * k2[None, :])) % W) / W
             cos, sin = np.cos(angle), np.sin(angle)
-            forward[j] = np.block([[cos, -sin], [sin, cos]])
-            inverse[j] = np.block([[cos.T, sin.T], [-sin.T, cos.T]]) * (2.0 / W)
-    return forward, inverse
+            table[j] = np.block([[cos, -sin], [sin, cos]])
+    return table
 
 
 def x_frequencies():
@@ -238,7 +234,8 @@
     angle_x = scale * (fx_ref[...] * fx_ref[...])
     cos_x, sin_x = jnp.cos(angle_x), jnp.sin(angle_x)
     for j in range(NJ):
-        gain_ref[j] = jnp.concatenate([cos_x[j : j + 1], sin_x[j : j + 1]], axis=0)
+        scaled = jnp.concatenate([cos_x[j : j + 1], sin_x[j : j + 1]], axis=0)
+        gain_ref[j] = scaled * ((1.0 if j == 0 else 2.0) / W)
     for odd in range(2):
         fy = fy_ref[odd : odd + 1, :]
         angle_y = scale * (fy * fy) + phase_shift
@@ -289,14 +286,32 @@
 
 NEAR_MB = 24
 MAIN_MB = 40
-BAND_MB = 16
 PROJECT_MB = 24
 
 
-def main_kernel(xa, xb, near, mix, gain, fh, fl, ih, il, out, vh, vl, eh, el, oh, ol, zh, zl, back):
-    load_strips((xa, xb), vh, vl)
-    for j in range(NJ):
-        far = three_products(vh[j], vl[j], fh[j], fl[j])
+def quarter_kernel(x_ref, fh, fl, out_ref, vh, vl):
+    load_strips((x_ref,), vh, vl)
+    for j in range(NJ):
+        out_ref[j] = three_products(vh[j], vl[j], fh[j], fl[j])
+
+
+def run_quarter(x, fh, fl):
+    return pl.pallas_call(
+        quarter_kernel,
+        in_specs=[vmem_spec()] * 3,
+        out_specs=vmem_spec(),
+        out_shape=jax.ShapeDtypeStruct((NJ, QUARTER, 2 * XQ), jnp.float32),
+        scratch_shapes=[pltpu.VMEM((NJ, QUARTER, 2 * XQ), jnp.bfloat16)] * 2,
+        compiler_params=parameters(NEAR_MB),
+        name="quarter",
+    )(x, fh, fl)
+
+
+def main_kernel(xb, near, quarter, mix, gain, fh, fl, out, vh, vl, eh, el, oh, ol, zh, zl, back):
+    load_strips((xb,), vh, vl)
+    for j in range(NJ):
+        last = three_products(vh[j], vl[j], fh[j], fl[j])
+        far = jnp.concatenate([quarter[j], last], axis=0)
         here = near[j]
         eh[j], el[j] = split(here + far)
         oh[j], ol[j] = split(here - far)
@@ -312,7 +327,11 @@
         even, odd = mixed(0, eh[j], el[j]), mixed(1, oh[j], ol[j])
         zh[j], zl[j] = split(jnp.concatenate([even + odd, even - odd], axis=0))
     for j in range(NJ):
-        back[j] = three_products(zh[j], zl[j], ih[j], il[j])
+        left = jnp.concatenate([zh[j], zl[j], zh[j]], axis=1)
+        right = jnp.concatenate([fh[j], fh[j], fl[j]], axis=1)
+        back[j] = lax.dot_general(
+            left, right, (((1,), (1,)), ((), ())), preferred_element_type=jnp.float32
+        )
 
     devices = TILTS // 2
     for half in range(2):
@@ -340,13 +359,14 @@
                         out[place, low_tile + tile] = joined.astype(jnp.bfloat16)
                 return carry
 
-            lax.fori_loop(0, devices // per_strip, strip, 0)
+            lax.fori_loop(0, devices // per_strip, strip, 0, unroll=4)
             low_row += devices * count
             low_tile += XP // per_tile
 
 
-def run_main(xa, xb, near, mix, gain, fh, fl, ih, il):
-    args = (xa, xb, near, mix, gain, fh, fl, ih, il)
+def run_main(xb, near, quarter, mix, gain, fh, fl):
+    args = (xb, near, quarter, mix, gain, fh, fl)
+    fourth = pltpu.VMEM((NJ, QUARTER, 2 * XQ), jnp.bfloat16)
     half = pltpu.VMEM((NJ, HALF, 2 * XQ), jnp.bfloat16)
     full = pltpu.VMEM((NJ, YB, 2 * XQ), jnp.bfloat16)
     return pl.pallas_call(
@@ -354,43 +374,13 @@
         in_specs=[vmem_spec()] * len(args),
         out_specs=vmem_spec(),
         out_shape=jax.ShapeDtypeStruct((TILTS, TILES, 16, XQ), jnp.bfloat16),
-        scratch_shapes=[half] * 6 + [full] * 2 + [pltpu.VMEM((NJ, YB, 2 * XQ), jnp.float32)],
+        scratch_shapes=[fourth] * 2 + [half] * 4 + [full] * 2 + [pltpu.VMEM((NJ, YB, 2 * XQ), jnp.float32)],
         compiler_params=parameters(MAIN_MB),
         name="main",
     )(*args)
 
 
-def band_kernel(off_ref, weight_ref, out_ref):
-    distance = lax.broadcasted_iota(jnp.int32, (2 * XQ, XQ), 0) - lax.broadcasted_iota(
-        jnp.int32, (2 * XQ, XQ), 1
-    )
-    distance = distance.astype(jnp.int16)
-
-    def tilt(t, carry):
-        for z in range(ZD):
-            shift = off_ref[t, z] & (XQ - 1)
-            band = jnp.zeros((2 * XQ, XQ), jnp.bfloat16)
-            for tap in range(TAPS):
-                weight = weight_ref[t, z * TAPS + tap].astype(jnp.bfloat16)
-                band = jnp.where(distance == (shift + tap).astype(jnp.int16), weight, band)
-            out_ref[t // GROUP, z, t % GROUP] = band
-        return carry
-
-    lax.fori_loop(0, TILTS, tilt, 0)
-
-
-def run_band(off, weights):
-    return pl.pallas_call(
-        band_kernel,
-        in_specs=[scalar_spec()] * 2,
-        out_specs=vmem_spec(),
-        out_shape=jax.ShapeDtypeStruct((TILTS // GROUP, ZD, GROUP, 2 * XQ, XQ), jnp.bfloat16),
-        compiler_params=parameters(BAND_MB),
-        name="bands",
-    )(off, weights)
-
-
-def project_kernel(off_ref, weight_ref, x, bands, out_ref, wide, narrow, total):
+def project_kernel(off_ref, weight_ref, x, out_ref, wide, narrow, total):
     wide[...] = jnp.zeros_like(wide)
     narrow[...] = jnp.zeros_like(narrow)
     total[...] = jnp.zeros_like(total)
@@ -408,6 +398,19 @@
             piece = padded[start & (per_tile - 1), g, pl.ds(start >> log_tile, tiles)]
             pieces.append(piece.reshape(tiles * 16, XQ))
         return jnp.concatenate(pieces, axis=0)
+
+    distance = lax.broadcasted_iota(jnp.int32, (2 * XQ, XQ), 0) - lax.broadcasted_iota(
+        jnp.int32, (2 * XQ, XQ), 1
+    )
+    distance = distance.astype(jnp.int16)
+
+    def band_of(t, z):
+        shift = off_ref[t, z] & (XQ - 1)
+        band = jnp.zeros((2 * XQ, XQ), jnp.bfloat16)
+        for tap in range(TAPS):
+            weight = weight_ref[t, z * TAPS + tap].astype(jnp.bfloat16)
+            band = jnp.where(distance == (shift + tap).astype(jnp.int16), weight, band)
+        return band
 
     def step(i, carry):
         late = 0
@@ -434,7 +437,7 @@
                 parts.append(window(g, start))
                 parts.append(window(g, start + 1))
             left = jnp.concatenate(parts, axis=1)
-            band = bands[i, z].reshape(GROUP * 2 * XQ, XQ)
+            band = jnp.concatenate([band_of(i * GROUP + g, z) for g in range(GROUP)], axis=0)
             total[z] += jnp.dot(left, band, preferred_element_type=jnp.float32)
 
         @pl.when(late > 0)
@@ -477,10 +480,10 @@
                 ]
 
 
-def run_project(off, weights, moved, bands):
+def run_project(off, weights, moved):
     return pl.pallas_call(
         project_kernel,
-        in_specs=[scalar_spec()] * 2 + [vmem_spec()] * 2,
+        in_specs=[scalar_spec()] * 2 + [vmem_spec()],
         out_specs=vmem_spec(),
         out_shape=jax.ShapeDtypeStruct((ROWS, ZD, W), jnp.float32),
         scratch_shapes=[
@@ -490,7 +493,7 @@
         ],
         compiler_params=parameters(PROJECT_MB),
         name="project",
-    )(off, weights, moved, bands)
+    )(off, weights, moved)
 
 
 def body(tilts, tilt_defocus, defocus_table, slab_pick, interp_offset, interp_weights):
@@ -504,17 +507,16 @@
     group_defocus = jnp.sum(jnp.where(entries == slab_pick[0], defocus_table, 0.0))
     focus = tilt_defocus + group_defocus
     slab = lax.axis_index("slab").astype(jnp.int32).reshape(1)
-    forward, inverse = x_tables()
-    fh, fl = (jnp.asarray(t) for t in split_np(forward))
-    ih, il = (jnp.asarray(t) for t in split_np(inverse))
+    fh, fl = (jnp.asarray(t) for t in split_np(x_table()))
     near, mix, gain = run_near(focus, slab, own, beside, fh, fl)
     near, across = lax.optimization_barrier((near, across))
     opposite = swap(across, 1)
     weights = interp_weights.astype(jnp.float32).reshape(TILTS, ZD * TAPS)
-    bands = run_band(interp_offset, weights)
-    filtered = run_main(across, opposite, near, mix, gain, fh, fl, ih, il)
+    quarter = run_quarter(across, fh, fl)
+    quarter, opposite = lax.optimization_barrier((quarter, opposite))
+    filtered = run_main(opposite, near, quarter, mix, gain, fh, fl)
     moved = lax.all_to_all(filtered, "dev", split_axis=0, concat_axis=0, tiled=True)
-    return run_project(interp_offset, weights, moved, bands)
+    return run_project(interp_offset, weights, moved)
 
 
 def solution(mesh):

time: 90.2 us -> 84.9 us (0.941); the launches traced: 89.7 us -> 83.3 us
  local copies, waits for them, and re-layouts: 15.6 us -> 9 us
  waiting for transfers between devices: 29.3 us -> 35.6 us
  Pallas kernels: 28.6 us -> 22.6 us
    all_to_all x1, waiting for transfers between devices: 26.8 us -> 34.4 us  [body(): lax.all_to_all(filtered, 'dev', split_axis=0, concat_axis=0, tiled=True)]
    unnamed x31 -> x25, local copies, waits for them, and re-layouts: 15.5 us -> 8.92 us
    pallas_call x1, Pallas kernels: 4.35 us -> 1.38 us  [run_quarter(): pl.pallas_call(quarter_kernel, in_specs=[vmem_spec()] * 3, out_specs=vmem...]
    pallas_call x1, Pallas kernels: 10.9 us -> 8.23 us  [run_main(): pl.pallas_call(main_kernel, in_specs=[vmem_spec()] * len(args), out_specs...]
    ppermute x3, waiting for transfers between devices: 2.5 us -> 1.27 us  [swap(): return lax.ppermute(block, 'slab', [(i, i ^ bit) for i in range(4)])]
  transfers between devices with their start and end apart: 4 -> 4, of which waited for: 3 -> 3; matrix products, arithmetic and copies ran while one was open for 2% -> 2% of each run, Pallas kernels for 8% -> 5%
where the time goes in v4:
time: 84.9 us; the launch traced here: 83.3 us
  waiting for transfers between devices  35.6 us (42%)
  Pallas kernels  22.6 us (27%)
  starting transfers between devices  12.8 us (15%)
  local copies, waits for them, and re-layouts  9 us (11%)
  between operations  2.01 us (2%)
  other arithmetic  1.28 us (2%)
    all_to_all x1, waiting for transfers between devices, body(): lax.all_to_all(filtered, 'dev', split_axis=0, concat_axis=0, tiled=True)  34.4 us
    all_to_all x1, starting transfers between devices, body(): lax.all_to_all(filtered, 'dev', split_axis=0, concat_axis=0, tiled=True)  10.9 us
    pallas_call x1, Pallas kernels, run_project(): pl.pallas_call(project_kernel, in_specs=[scalar_spec()] * 2 + [vmem_spec(...  10.1 us
    unnamed x25, local copies, waits for them, and re-layouts  8.92 us
    pallas_call x1, Pallas kernels, run_main(): pl.pallas_call(main_kernel, in_specs=[vmem_spec()] * len(args), out_specs...  8.23 us
    pallas_call x1, Pallas kernels, run_near(): pl.pallas_call(near_kernel, in_specs=[scalar_spec()] * 2 + [vmem_spec()]...  2.9 us
    ppermute x3, starting transfers between devices, swap(): return lax.ppermute(block, 'slab', [(i, i ^ bit) for i in range(4)])  1.92 us
  transfers between devices with their start and end apart: 4, of which 3 were waited for; matrix products, arithmetic and copies ran while one was open for 2% of the time, Pallas kernels for 5%

profile of v4, /device:TPU:2, one launch (start us, length us, event | category | flops | bytes accessed | tf_op | source)
XLA Modules:
  0.0 83.3 jit_solution(3502311456633507940)
XLA Ops:
  0.0 0.0 collective-permute-start
  0.0 1.9 %collective-permute-start.1 = (bf16[96,3072]{1,0:T(8,128)(2,1)}, bf16[96,3072]{1,0:T(8,128)(2,1)S(1)}, u32[]{:S(2)}, u32[]{:S(2)}) collective-permute-start(bf16[96,3072]{1,0:T(8,128)(2,1)} %bitcast.8), channel_id=1, source_target_pairs={{0,64},{32,96},{64,0},{96,32},{1,65},{33,97},{65,1},{97,33},{2,66}... | collective-permute-start | bytes 1769480 | tf_op jit(solution)/shard_map/ppermute | solution.py:501
  3.2 1.3 %fusion = f32[]{:T(128)} fusion(f32[8]{0:T(128)} %param.14, s32[]{:T(128)} %bitcast.6), kind=kLoop, calls=%fused_computation.1 | loop fusion | flops 23 | bytes 40 | tf_op jit(solution)/shard_map/reduce_sum | solution.py:507
  5.1 0.0 collective-permute-done.xb_ref
  5.2 0.0 copy-start
  5.2 1.4 %copy-done = bf16[12,256,256]{2,1,0:T(8,128)(2,1)S(1)} copy-done((bf16[12,256,256]{2,1,0:T(8,128)(2,1)S(1)}, bf16[12,256,256]{2,1,0:T(8,128)(2,1)}, u32[]{:S(2)}) %copy-start) | copy-done | bytes 1572888
  6.6 1.4 %copy-done.2 = bf16[12,256,256]{2,1,0:T(8,128)(2,1)S(1)} copy-done((bf16[12,256,256]{2,1,0:T(8,128)(2,1)S(1)}, bf16[12,256,256]{2,1,0:T(8,128)(2,1)}, u32[]{:S(2)}) %copy-start.2) | copy-done | bytes 1572888
  8.0 1.1 %copy-done.5 = f32[2,2,192,192]{3,2,1,0:T(8,128)S(1)} copy-done((f32[2,2,192,192]{3,2,1,0:T(8,128)S(1)}, f32[2,2,192,192]{3,2,1,0:T(8,128)}, u32[]{:S(2)}) %copy-start.5) | copy-done | bytes 589848
  9.1 1.1 %copy-done.6 = bf16[1,96,3072]{2,1,0:T(8,128)(2,1)S(1)} copy-done((bf16[1,96,3072]{2,1,0:T(8,128)(2,1)S(1)}, bf16[1,96,3072]{2,1,0:T(8,128)(2,1)}, u32[]{:S(2)}) %copy-start.6) | copy-done | bytes 589848
  10.2 1.0 %copy-done.7 = f32[2,192,192]{2,1,0:T(8,128)S(1)} copy-done((f32[2,192,192]{2,1,0:T(8,128)S(1)}, f32[2,192,192]{2,1,0:T(8,128)}, u32[]{:S(2)}) %copy-start.7) | copy-done | bytes 294936
  11.2 0.7 copy-done.8
  11.9 0.7 copy-done.9
  12.6 2.9 %near.1 = (f32[12,192,256]{2,1,0:T(8,128)S(1)}, bf16[2,384,768]{2,1,0:T(8,128)(2,1)S(1)}, f32[12,2,256]{2,1,0:T(2,128)S(1)}) custom-call(f32[1]{0:T(128)S(6)} %add.7.focus_ref, s32[1]{0:T(128)} %bitcast.3.slab_ref, bf16[96,3072]{1,0:T(8,128)(2,1)S(1)} %bitcast.9, bf16[96,3072]{1,0:T(8,128)(2,1)S(1)} %collective-permute-done.xb_ref, ...), custom_call_target="tpu_custom_call" | custom-call | tf_op jit(solution)/shard_map/near/pallas_call | solution.py:272
  15.5 0.6 collective-permute-done.1.x_ref
  16.1 0.0 collective-permute-start.2
  16.1 1.4 %quarter.1 = f32[12,96,256]{2,1,0:T(8,128)S(1)} custom-call(bf16[96,3072]{1,0:T(8,128)(2,1)S(1)} %collective-permute-done.1.x_ref, bf16[12,256,256]{2,1,0:T(8,128)(2,1)S(1)} %copy-done.1, bf16[12,256,256]{2,1,0:T(8,128)(2,1)S(1)} %copy-done.3), custom_call_target="tpu_custom_call" | custom-call | tf_op jit(solution)/shard_map/quarter/pallas_call | solution.py:299
  17.5 0.6 collective-permute-done.2.xb
  18.1 8.2 %main.1 = bf16[32,18,16,128]{3,2,1,0:T(8,128)(2,1)S(1)} custom-call(bf16[96,3072]{1,0:T(8,128)(2,1)S(1)} %collective-permute-done.2.xb, f32[12,192,256]{2,1,0:T(8,128)S(1)} %get-tuple-element.15.near, f32[12,96,256]{2,1,0:T(8,128)S(1)} %quarter.1, bf16[2,384,768]{2,1,0:T(8,128)(2,1)S(1)} %get-tuple-element.17.mix, f32[12,2,256]{2,1,0:T(2,128)S(1)} %get-tuple-element.18.gain, ...), custom_call_target="tpu_custom_call" | custom-call | tf_op jit(solution)/shard_map/main/pallas_call | solution.py:372
  26.4 1.4 %copy-done.4 = bf16[32,18,16,128]{3,2,1,0:T(8,128)(2,1)} copy-done((bf16[32,18,16,128]{3,2,1,0:T(8,128)(2,1)}, bf16[32,18,16,128]{3,2,1,0:T(8,128)(2,1)S(1)}, u32[]{:S(2)}) %copy-start.4) | copy-done | bytes 2359320
  27.8 10.9 %all-to-all-start = ((bf16[32,18,16,128]{3,2,1,0:T(8,128)(2,1)}), bf16[32,18,16,128]{3,2,1,0:T(8,128)(2,1)S(1)}, u32[]{:S(2)}, u32[]{:S(2)}) async-start(bf16[32,18,16,128]{3,2,1,0:T(8,128)(2,1)} %copy-done.4), calls=%async_computation | async-start | bytes 4718592 | tf_op jit(solution)/shard_map/all_to_all | solution.py:518
  38.7 0.1 copy.15.off_ref
  38.8 0.1 copy.16.weight_ref
  38.9 34.4 %all-to-all-done.x = bf16[32,18,16,128]{3,2,1,0:T(8,128)(2,1)S(1)} async-done(((bf16[32,18,16,128]{3,2,1,0:T(8,128)(2,1)}), bf16[32,18,16,128]{3,2,1,0:T(8,128)(2,1)S(1)}, u32[]{:S(2)}, u32[]{:S(2)}) %all-to-all-start) | async-done | bytes 2359328 | tf_op jit(solution)/shard_map/all_to_all | solution.py:518
  73.3 10.1 %project.1 = f32[12,4,3072]{2,1,0:T(4,128)} custom-call(s32[32,4]{1,0:T(8,128)S(1)} %copy.15.off_ref, f32[32,16]{1,0:T(8,128)S(1)} %copy.16.weight_ref, bf16[32,18,16,128]{3,2,1,0:T(8,128)(2,1)S(1)} %all-to-all-done.x), custom_call_target="tpu_custom_call" | custom-call | tf_op jit(solution)/shard_map/project/pallas_call | solution.py:484
  (15 shorter events, 0.0 us)
Async XLA Ops:
  0.0 5.1 %collective-permute-start = (bf16[96,3072]{1,0:T(8,128)(2,1)}, bf16[96,3072]{1,0:T(8,128)(2,1)S(1)}, u32[]{:S(2)}, u32[]{:S(2)}) collective-permute-start(bf16[96,3072]{1,0:T(8,128)(2,1)} %bitcast.7), channel_id=1, source_target_pairs={{0,32},{32,0},{64,96},{96,64},{1,33},{33,1},{65,97},{97,65},{2,34}... | collective-permute-start | bytes 1769480 | tf_op jit(solution)/shard_map/ppermute | solution.py:501
  0.0 16.1 %collective-permute-start.1 = (bf16[96,3072]{1,0:T(8,128)(2,1)}, bf16[96,3072]{1,0:T(8,128)(2,1)S(1)}, u32[]{:S(2)}, u32[]{:S(2)}) collective-permute-start(bf16[96,3072]{1,0:T(8,128)(2,1)} %bitcast.8), channel_id=1, source_target_pairs={{0,64},{32,96},{64,0},{96,32},{1,65},{33,97},{65,1},{97,33},{2,66}... | collective-permute-start | bytes 1769480 | tf_op jit(solution)/shard_map/ppermute | solution.py:501
  5.2 1.4 %copy-start = (bf16[12,256,256]{2,1,0:T(8,128)(2,1)S(1)}, bf16[12,256,256]{2,1,0:T(8,128)(2,1)}, u32[]{:S(2)}) copy-start(bf16[12,256,256]{2,1,0:T(8,128)(2,1)} %constant.20.clone.fh) | copy-start | bytes 4718596
  6.6 1.4 %copy-start.2 = (bf16[12,256,256]{2,1,0:T(8,128)(2,1)S(1)}, bf16[12,256,256]{2,1,0:T(8,128)(2,1)}, u32[]{:S(2)}) copy-start(bf16[12,256,256]{2,1,0:T(8,128)(2,1)} %constant.21.clone.fl) | copy-start | bytes 4718596
  8.0 1.1 %copy-start.5 = (f32[2,2,192,192]{3,2,1,0:T(8,128)S(1)}, f32[2,2,192,192]{3,2,1,0:T(8,128)}, u32[]{:S(2)}) copy-start(f32[2,2,192,192]{3,2,1,0:T(8,128)} %constant.23.clone.right_ref) | copy-start | bytes 1769476
  9.1 1.1 %copy-start.6 = (bf16[1,96,3072]{2,1,0:T(8,128)(2,1)S(1)}, bf16[1,96,3072]{2,1,0:T(8,128)(2,1)}, u32[]{:S(2)}) copy-start(bf16[1,96,3072]{2,1,0:T(8,128)(2,1)} %param.12) | copy-start | bytes 1769476
  10.2 1.0 %copy-start.7 = (f32[2,192,192]{2,1,0:T(8,128)S(1)}, f32[2,192,192]{2,1,0:T(8,128)}, u32[]{:S(2)}) copy-start(f32[2,192,192]{2,1,0:T(8,128)} %constant.22.clone.left_ref) | copy-start | bytes 884740
  11.2 0.7 copy-start.8
  11.9 0.7 copy-start.9
  12.6 3.6 %copy-start.1 = (bf16[12,256,256]{2,1,0:T(8,128)(2,1)S(1)}, bf16[12,256,256]{2,1,0:T(8,128)(2,1)}, u32[]{:S(2)}) copy-start(bf16[12,256,256]{2,1,0:T(8,128)(2,1)} %constant.20.clone.fh) | copy-start | bytes 4718596
  12.6 3.6 %copy-start.3 = (bf16[12,256,256]{2,1,0:T(8,128)(2,1)S(1)}, bf16[12,256,256]{2,1,0:T(8,128)(2,1)}, u32[]{:S(2)}) copy-start(bf16[12,256,256]{2,1,0:T(8,128)(2,1)} %constant.21.clone.fl) | copy-start | bytes 4718596
  16.1 2.0 %collective-permute-start.2 = (bf16[96,3072]{1,0:T(8,128)(2,1)S(1)}, bf16[96,3072]{1,0:T(8,128)(2,1)S(1)}, u32[]{:S(2)}, u32[]{:S(2)}) collective-permute-start(bf16[96,3072]{1,0:T(8,128)(2,1)S(1)} %collective-permute-done.1.x_ref), channel_id=1, source_target_pairs={{0,32},{32,0},{64,96},{96,64},{1,33},{33,1},{65,97},{97,65},{2,34}... | collective-permute-start | bytes 1769480 | tf_op jit(solution)/shard_map/ppermute | solution.py:501
  26.4 1.4 %copy-start.4 = (bf16[32,18,16,128]{3,2,1,0:T(8,128)(2,1)}, bf16[32,18,16,128]{3,2,1,0:T(8,128)(2,1)S(1)}, u32[]{:S(2)}) copy-start(bf16[32,18,16,128]{3,2,1,0:T(8,128)(2,1)S(1)} %main.1) | copy-start | bytes 7077892
  27.8 10.9 %copy-start.11 = (s32[32,4]{0,1:T(4,128)S(1)}, s32[32,4]{0,1:T(4,128)}, u32[]{:S(2)}) copy-start(s32[32,4]{0,1:T(4,128)} %param.16) | copy-start | bytes 1540
  27.8 11.0 %copy-start.10 = (bf16[32,4,4]{0,2,1:T(4,128)(2,1)S(1)}, bf16[32,4,4]{0,2,1:T(4,128)(2,1)}, u32[]{:S(2)}) copy-start(bf16[32,4,4]{0,2,1:T(4,128)(2,1)} %param.17) | copy-start | bytes 3076
  27.8 45.5 %all-to-all-start = ((bf16[32,18,16,128]{3,2,1,0:T(8,128)(2,1)}), bf16[32,18,16,128]{3,2,1,0:T(8,128)(2,1)S(1)}, u32[]{:S(2)}, u32[]{:S(2)}) async-start(bf16[32,18,16,128]{3,2,1,0:T(8,128)(2,1)} %copy-done.4), calls=%async_computation | async-start | bytes 4718592 | tf_op jit(solution)/shard_map/all_to_all | solution.py:518

commit v5 on v4

--- a/solution.py
+++ b/solution.py
@@ -56,20 +56,20 @@
     return table
 
 
+def frequency(index, count):
+    return jnp.where(2 * index < count, index, index - count).astype(jnp.float32) / count
+
+
 def x_frequencies():
-    k2 = np.arange(XQ)
-    result = np.zeros((NJ, 2 * XQ))
-    for j in range(NJ):
-        first, second = (0, 12) if j == 0 else (j, j)
-        for half, k1 in enumerate((first, second)):
-            k = k1 + XP * k2
-            result[j, half * XQ : (half + 1) * XQ] = np.where(2 * k < W, k, k - W) / W
-    return result
-
-
-def y_frequencies():
-    a = np.arange(YB)
-    return np.where(2 * a < YB, a, a - YB) / YB
+    shape = (NJ, 2 * XQ)
+    j = lax.broadcasted_iota(jnp.int32, shape, 0)
+    place = lax.broadcasted_iota(jnp.int32, shape, 1)
+    k1 = jnp.where(j == 0, jnp.where(place < XQ, 0, XP // 2), j)
+    return frequency(k1 + XP * (place & (XQ - 1)), W)
+
+
+def y_frequencies(odd):
+    return frequency(2 * lax.broadcasted_iota(jnp.int32, (1, HALF), 1) + odd, YB)
 
 
 def y_tables():
@@ -224,20 +224,21 @@
         lax.fori_loop(0, QUARTER // STRIP, strip, 0)
 
 
-def near_kernel(focus_ref, slab_ref, xa_ref, xb_ref, fh, fl, left_ref, right_ref, fy_ref, fx_ref,
-                out_ref, mix_ref, gain_ref, vh, vl):
+def near_kernel(focus_ref, slab_ref, xa_ref, xb_ref, fh, fl, left_ref, right_ref, out_ref, mix_ref,
+                gain_ref, vh, vl):
     load_strips((xa_ref, xb_ref), vh, vl)
     for j in range(NJ):
         out_ref[j] = three_products(vh[j], vl[j], fh[j], fl[j])
     scale = chi_scale * focus_ref[0]
     slab = slab_ref[0]
-    angle_x = scale * (fx_ref[...] * fx_ref[...])
+    fx = x_frequencies()
+    angle_x = scale * (fx * fx)
     cos_x, sin_x = jnp.cos(angle_x), jnp.sin(angle_x)
     for j in range(NJ):
         scaled = jnp.concatenate([cos_x[j : j + 1], sin_x[j : j + 1]], axis=0)
         gain_ref[j] = scaled * ((1.0 if j == 0 else 2.0) / W)
     for odd in range(2):
-        fy = fy_ref[odd : odd + 1, :]
+        fy = y_frequencies(odd)
         angle_y = scale * (fy * fy) + phase_shift
         left = left_ref[odd]
         side = jnp.concatenate([left * -jnp.sin(angle_y), left * -jnp.cos(angle_y)], axis=0)
@@ -266,12 +267,9 @@
 
 def run_near(focus, slab, xa, xb, fh, fl):
     left, right = y_tables()
-    fy = y_frequencies()
-    fy = np.stack([fy[0::2], fy[1::2]]).astype(np.float32)
-    fx = x_frequencies().astype(np.float32)
     return pl.pallas_call(
         near_kernel,
-        in_specs=[scalar_spec()] * 2 + [vmem_spec()] * 8,
+        in_specs=[scalar_spec()] * 2 + [vmem_spec()] * 6,
         out_specs=[vmem_spec()] * 3,
         out_shape=[
             jax.ShapeDtypeStruct((NJ, HALF, 2 * XQ), jnp.float32),
@@ -281,7 +279,7 @@
         scratch_shapes=[pltpu.VMEM((NJ, HALF, 2 * XQ), jnp.bfloat16)] * 2,
         compiler_params=parameters(NEAR_MB),
         name="near",
-    )(focus, slab, xa, xb, fh, fl, *(jnp.asarray(t) for t in (left, right, fy, fx)))
+    )(focus, slab, xa, xb, fh, fl, jnp.asarray(left), jnp.asarray(right))
 
 
 NEAR_MB = 24
@@ -307,7 +305,7 @@
     )(x, fh, fl)
 
 
-def main_kernel(xb, near, quarter, mix, gain, fh, fl, out, vh, vl, eh, el, oh, ol, zh, zl, back):
+def main_kernel(xb, near, quarter, mix, gain, fh, fl, ih, il, out, vh, vl, eh, el, oh, ol, zh, zl, back):
     load_strips((xb,), vh, vl)
     for j in range(NJ):
         last = three_products(vh[j], vl[j], fh[j], fl[j])
@@ -328,10 +326,8 @@
         zh[j], zl[j] = split(jnp.concatenate([even + odd, even - odd], axis=0))
     for j in range(NJ):
         left = jnp.concatenate([zh[j], zl[j], zh[j]], axis=1)
-        right = jnp.concatenate([fh[j], fh[j], fl[j]], axis=1)
-        back[j] = lax.dot_general(
-            left, right, (((1,), (1,)), ((), ())), preferred_element_type=jnp.float32
-        )
+        right = jnp.concatenate([ih[j], ih[j], il[j]], axis=0)
+        back[j] = jnp.dot(left, right, preferred_element_type=jnp.float32)
 
     devices = TILTS // 2
     for half in range(2):
@@ -364,8 +360,8 @@
             low_tile += XP // per_tile
 
 
-def run_main(xb, near, quarter, mix, gain, fh, fl):
-    args = (xb, near, quarter, mix, gain, fh, fl)
+def run_main(xb, near, quarter, mix, gain, fh, fl, ih, il):
+    args = (xb, near, quarter, mix, gain, fh, fl, ih, il)
     fourth = pltpu.VMEM((NJ, QUARTER, 2 * XQ), jnp.bfloat16)
     half = pltpu.VMEM((NJ, HALF, 2 * XQ), jnp.bfloat16)
     full = pltpu.VMEM((NJ, YB, 2 * XQ), jnp.bfloat16)
@@ -501,20 +497,21 @@
         return lax.ppermute(block, "slab", [(i, i ^ bit) for i in range(4)])
 
     own = tilts[0]
+    across = swap(own, 2)
     beside = swap(own, 1)
-    across = swap(own, 2)
     entries = jnp.arange(defocus_table.shape[0], dtype=jnp.int32)
     group_defocus = jnp.sum(jnp.where(entries == slab_pick[0], defocus_table, 0.0))
     focus = tilt_defocus + group_defocus
     slab = lax.axis_index("slab").astype(jnp.int32).reshape(1)
     fh, fl = (jnp.asarray(t) for t in split_np(x_table()))
+    ih, il = (jnp.asarray(t) for t in split_np(np.swapaxes(x_table(), 1, 2)))
     near, mix, gain = run_near(focus, slab, own, beside, fh, fl)
     near, across = lax.optimization_barrier((near, across))
     opposite = swap(across, 1)
     weights = interp_weights.astype(jnp.float32).reshape(TILTS, ZD * TAPS)
     quarter = run_quarter(across, fh, fl)
     quarter, opposite = lax.optimization_barrier((quarter, opposite))
-    filtered = run_main(opposite, near, quarter, mix, gain, fh, fl)
+    filtered = run_main(opposite, near, quarter, mix, gain, fh, fl, ih, il)
     moved = lax.all_to_all(filtered, "dev", split_axis=0, concat_axis=0, tiled=True)
     return run_project(interp_offset, weights, moved)
 

time: 84.9 us -> 84.3 us (level)
  waiting for transfers between devices: 35.6 us -> 37 us
  local copies, waits for them, and re-layouts: 9 us -> 7.61 us
    unnamed x25, local copies, waits for them, and re-layouts: 8.92 us -> 7.53 us
    ppermute x3, waiting for transfers between devices: 1.27 us -> 2.61 us  [swap(): return lax.ppermute(block, 'slab', [(i, i ^ bit) for i in range(4)])]
where the time goes in v5:
time: 84.3 us; the launch traced here: 83.3 us
  waiting for transfers between devices  37 us (44%)
  Pallas kernels  22.6 us (27%)
  starting transfers between devices  12.8 us (15%)
  local copies, waits for them, and re-layouts  7.61 us (9%)
  between operations  2.02 us (2%)
  other arithmetic  1.28 us (2%)
    all_to_all x1, waiting for transfers between devices, body(): lax.all_to_all(filtered, 'dev', split_axis=0, concat_axis=0, tiled=True)  34.4 us
    all_to_all x1, starting transfers between devices, body(): lax.all_to_all(filtered, 'dev', split_axis=0, concat_axis=0, tiled=True)  10.9 us
    pallas_call x1, Pallas kernels, run_project(): pl.pallas_call(project_kernel, in_specs=[scalar_spec()] * 2 + [vmem_spec(...  10 us
    pallas_call x1, Pallas kernels, run_main(): pl.pallas_call(main_kernel, in_specs=[vmem_spec()] * len(args), out_specs...  8.24 us
    unnamed x25, local copies, waits for them, and re-layouts  7.53 us
    pallas_call x1, Pallas kernels, run_near(): pl.pallas_call(near_kernel, in_specs=[scalar_spec()] * 2 + [vmem_spec()]...  2.95 us
    ppermute x3, waiting for transfers between devices, swap(): return lax.ppermute(block, 'slab', [(i, i ^ bit) for i in range(4)])  2.61 us
    ppermute x3, starting transfers between devices, swap(): return lax.ppermute(block, 'slab', [(i, i ^ bit) for i in range(4)])  1.92 us
  transfers between devices with their start and end apart: 4, of which 3 were waited for; matrix products, arithmetic and copies ran while one was open for 2% of the time, Pallas kernels for 5%

profile of v5, /device:TPU:2, one launch (start us, length us, event | category | flops | bytes accessed | tf_op | source)
XLA Modules:
  0.0 83.3 jit_solution(376448938312034622)
XLA Ops:
  0.0 0.0 collective-permute-start
  0.0 1.9 %collective-permute-start.1 = (bf16[96,3072]{1,0:T(8,128)(2,1)}, bf16[96,3072]{1,0:T(8,128)(2,1)S(1)}, u32[]{:S(2)}, u32[]{:S(2)}) collective-permute-start(bf16[96,3072]{1,0:T(8,128)(2,1)} %bitcast.8), channel_id=1, source_target_pairs={{0,64},{32,96},{64,0},{96,32},{1,65},{33,97},{65,1},{97,33},{2,66}... | collective-permute-start | bytes 1769480 | tf_op jit(solution)/shard_map/ppermute | solution.py:497
  3.2 1.3 %fusion = f32[]{:T(128)} fusion(f32[8]{0:T(128)} %param.14, s32[]{:T(128)} %bitcast.6), kind=kLoop, calls=%fused_computation.1 | loop fusion | flops 23 | bytes 40 | tf_op jit(solution)/shard_map/reduce_sum | solution.py:503
  5.1 0.0 collective-permute-done.xb_ref
  5.2 0.0 copy-start
  5.2 1.4 %copy-done = bf16[12,256,256]{2,1,0:T(8,128)(2,1)S(1)} copy-done((bf16[12,256,256]{2,1,0:T(8,128)(2,1)S(1)}, bf16[12,256,256]{2,1,0:T(8,128)(2,1)}, u32[]{:S(2)}) %copy-start) | copy-done | bytes 1572888
  6.6 1.4 %copy-done.2 = bf16[12,256,256]{2,1,0:T(8,128)(2,1)S(1)} copy-done((bf16[12,256,256]{2,1,0:T(8,128)(2,1)S(1)}, bf16[12,256,256]{2,1,0:T(8,128)(2,1)}, u32[]{:S(2)}) %copy-start.2) | copy-done | bytes 1572888
  8.0 1.1 %copy-done.7 = f32[2,2,192,192]{3,2,1,0:T(8,128)S(1)} copy-done((f32[2,2,192,192]{3,2,1,0:T(8,128)S(1)}, f32[2,2,192,192]{3,2,1,0:T(8,128)}, u32[]{:S(2)}) %copy-start.7) | copy-done | bytes 589848
  9.1 1.1 %copy-done.8 = bf16[1,96,3072]{2,1,0:T(8,128)(2,1)S(1)} copy-done((bf16[1,96,3072]{2,1,0:T(8,128)(2,1)S(1)}, bf16[1,96,3072]{2,1,0:T(8,128)(2,1)}, u32[]{:S(2)}) %copy-start.8) | copy-done | bytes 589848
  10.2 1.0 %copy-done.9 = f32[2,192,192]{2,1,0:T(8,128)S(1)} copy-done((f32[2,192,192]{2,1,0:T(8,128)S(1)}, f32[2,192,192]{2,1,0:T(8,128)}, u32[]{:S(2)}) %copy-start.9) | copy-done | bytes 294936
  11.2 2.9 %near.1 = (f32[12,192,256]{2,1,0:T(8,128)S(1)}, bf16[2,384,768]{2,1,0:T(8,128)(2,1)S(1)}, f32[12,2,256]{2,1,0:T(2,128)S(1)}) custom-call(f32[1]{0:T(128)S(6)} %add.7.focus_ref, s32[1]{0:T(128)} %bitcast.3.slab_ref, bf16[96,3072]{1,0:T(8,128)(2,1)S(1)} %bitcast.9, bf16[96,3072]{1,0:T(8,128)(2,1)S(1)} %collective-permute-done.xb_ref, ...), custom_call_target="tpu_custom_call" | custom-call | tf_op jit(solution)/shard_map/near/pallas_call | solution.py:270
  14.1 2.0 %collective-permute-done.1.x_ref = bf16[96,3072]{1,0:T(8,128)(2,1)S(1)} collective-permute-done((bf16[96,3072]{1,0:T(8,128)(2,1)}, bf16[96,3072]{1,0:T(8,128)(2,1)S(1)}, u32[]{:S(2)}, u32[]{:S(2)}) %collective-permute-start.1) | collective-permute-done | bytes 589856 | tf_op jit(solution)/shard_map/ppermute | solution.py:497
  16.1 0.0 collective-permute-start.2
  16.1 0.0 copy-done.1
  16.1 0.0 copy-done.3
  16.2 1.4 %quarter.1 = f32[12,96,256]{2,1,0:T(8,128)S(1)} custom-call(bf16[96,3072]{1,0:T(8,128)(2,1)S(1)} %collective-permute-done.1.x_ref, bf16[12,256,256]{2,1,0:T(8,128)(2,1)S(1)} %copy-done.1, bf16[12,256,256]{2,1,0:T(8,128)(2,1)S(1)} %copy-done.3), custom_call_target="tpu_custom_call" | custom-call | tf_op jit(solution)/shard_map/quarter/pallas_call | solution.py:297
  17.5 0.6 collective-permute-done.2.xb
  18.1 8.2 %main.1 = bf16[32,18,16,128]{3,2,1,0:T(8,128)(2,1)S(1)} custom-call(bf16[96,3072]{1,0:T(8,128)(2,1)S(1)} %collective-permute-done.2.xb, f32[12,192,256]{2,1,0:T(8,128)S(1)} %get-tuple-element.15.near, f32[12,96,256]{2,1,0:T(8,128)S(1)} %quarter.1, bf16[2,384,768]{2,1,0:T(8,128)(2,1)S(1)} %get-tuple-element.17.mix, f32[12,2,256]{2,1,0:T(2,128)S(1)} %get-tuple-element.18.gain, ...), custom_call_target="tpu_custom_call" | custom-call | tf_op jit(solution)/shard_map/main/pallas_call | solution.py:368
  26.4 1.4 %copy-done.4 = bf16[32,18,16,128]{3,2,1,0:T(8,128)(2,1)} copy-done((bf16[32,18,16,128]{3,2,1,0:T(8,128)(2,1)}, bf16[32,18,16,128]{3,2,1,0:T(8,128)(2,1)S(1)}, u32[]{:S(2)}) %copy-start.4) | copy-done | bytes 2359320
  27.8 10.9 %all-to-all-start = ((bf16[32,18,16,128]{3,2,1,0:T(8,128)(2,1)}), bf16[32,18,16,128]{3,2,1,0:T(8,128)(2,1)S(1)}, u32[]{:S(2)}, u32[]{:S(2)}) async-start(bf16[32,18,16,128]{3,2,1,0:T(8,128)(2,1)} %copy-done.4), calls=%async_computation | async-start | bytes 4718592 | tf_op jit(solution)/shard_map/all_to_all | solution.py:515
  38.7 0.1 copy.15.off_ref
  38.8 0.1 copy.16.weight_ref
  38.9 34.4 %all-to-all-done.x = bf16[32,18,16,128]{3,2,1,0:T(8,128)(2,1)S(1)} async-done(((bf16[32,18,16,128]{3,2,1,0:T(8,128)(2,1)}), bf16[32,18,16,128]{3,2,1,0:T(8,128)(2,1)S(1)}, u32[]{:S(2)}, u32[]{:S(2)}) %all-to-all-start) | async-done | bytes 2359328 | tf_op jit(solution)/shard_map/all_to_all | solution.py:515
  73.3 10.0 %project.1 = f32[12,4,3072]{2,1,0:T(4,128)} custom-call(s32[32,4]{1,0:T(8,128)S(1)} %copy.15.off_ref, f32[32,16]{1,0:T(8,128)S(1)} %copy.16.weight_ref, bf16[32,18,16,128]{3,2,1,0:T(8,128)(2,1)S(1)} %all-to-all-done.x), custom_call_target="tpu_custom_call" | custom-call | tf_op jit(solution)/shard_map/project/pallas_call | solution.py:480
  (15 shorter events, 0.0 us)
Async XLA Ops:
  0.0 5.1 %collective-permute-start = (bf16[96,3072]{1,0:T(8,128)(2,1)}, bf16[96,3072]{1,0:T(8,128)(2,1)S(1)}, u32[]{:S(2)}, u32[]{:S(2)}) collective-permute-start(bf16[96,3072]{1,0:T(8,128)(2,1)} %bitcast.7), channel_id=1, source_target_pairs={{0,32},{32,0},{64,96},{96,64},{1,33},{33,1},{65,97},{97,65},{2,34}... | collective-permute-start | bytes 1769480 | tf_op jit(solution)/shard_map/ppermute | solution.py:497
  0.0 16.1 %collective-permute-start.1 = (bf16[96,3072]{1,0:T(8,128)(2,1)}, bf16[96,3072]{1,0:T(8,128)(2,1)S(1)}, u32[]{:S(2)}, u32[]{:S(2)}) collective-permute-start(bf16[96,3072]{1,0:T(8,128)(2,1)} %bitcast.8), channel_id=1, source_target_pairs={{0,64},{32,96},{64,0},{96,32},{1,65},{33,97},{65,1},{97,33},{2,66}... | collective-permute-start | bytes 1769480 | tf_op jit(solution)/shard_map/ppermute | solution.py:497
  5.2 1.4 %copy-start = (bf16[12,256,256]{2,1,0:T(8,128)(2,1)S(1)}, bf16[12,256,256]{2,1,0:T(8,128)(2,1)}, u32[]{:S(2)}) copy-start(bf16[12,256,256]{2,1,0:T(8,128)(2,1)} %constant.20.clone.fh) | copy-start | bytes 4718596
  6.6 1.4 %copy-start.2 = (bf16[12,256,256]{2,1,0:T(8,128)(2,1)S(1)}, bf16[12,256,256]{2,1,0:T(8,128)(2,1)}, u32[]{:S(2)}) copy-start(bf16[12,256,256]{2,1,0:T(8,128)(2,1)} %constant.21.clone.fl) | copy-start | bytes 4718596
  8.0 1.1 %copy-start.7 = (f32[2,2,192,192]{3,2,1,0:T(8,128)S(1)}, f32[2,2,192,192]{3,2,1,0:T(8,128)}, u32[]{:S(2)}) copy-start(f32[2,2,192,192]{3,2,1,0:T(8,128)} %constant.25.clone.right_ref) | copy-start | bytes 1769476
  9.1 1.1 %copy-start.8 = (bf16[1,96,3072]{2,1,0:T(8,128)(2,1)S(1)}, bf16[1,96,3072]{2,1,0:T(8,128)(2,1)}, u32[]{:S(2)}) copy-start(bf16[1,96,3072]{2,1,0:T(8,128)(2,1)} %param.12) | copy-start | bytes 1769476
  10.2 1.0 %copy-start.9 = (f32[2,192,192]{2,1,0:T(8,128)S(1)}, f32[2,192,192]{2,1,0:T(8,128)}, u32[]{:S(2)}) copy-start(f32[2,192,192]{2,1,0:T(8,128)} %constant.24.clone.left_ref) | copy-start | bytes 884740
  11.2 5.0 %copy-start.1 = (bf16[12,256,256]{2,1,0:T(8,128)(2,1)S(1)}, bf16[12,256,256]{2,1,0:T(8,128)(2,1)}, u32[]{:S(2)}) copy-start(bf16[12,256,256]{2,1,0:T(8,128)(2,1)} %constant.20.clone.fh) | copy-start | bytes 4718596
  11.2 5.0 %copy-start.3 = (bf16[12,256,256]{2,1,0:T(8,128)(2,1)S(1)}, bf16[12,256,256]{2,1,0:T(8,128)(2,1)}, u32[]{:S(2)}) copy-start(bf16[12,256,256]{2,1,0:T(8,128)(2,1)} %constant.21.clone.fl) | copy-start | bytes 4718596
  16.1 2.0 %copy-start.5 = (bf16[12,256,256]{2,1,0:T(8,128)(2,1)S(1)}, bf16[12,256,256]{2,1,0:T(8,128)(2,1)}, u32[]{:S(2)}) copy-start(bf16[12,256,256]{2,1,0:T(8,128)(2,1)} %constant.22.clone.ih) | copy-start | bytes 4718596
  16.1 2.0 %copy-start.6 = (bf16[12,256,256]{2,1,0:T(8,128)(2,1)S(1)}, bf16[12,256,256]{2,1,0:T(8,128)(2,1)}, u32[]{:S(2)}) copy-start(bf16[12,256,256]{2,1,0:T(8,128)(2,1)} %constant.23.clone.il) | copy-start | bytes 4718596
  16.1 2.0 %collective-permute-start.2 = (bf16[96,3072]{1,0:T(8,128)(2,1)S(1)}, bf16[96,3072]{1,0:T(8,128)(2,1)S(1)}, u32[]{:S(2)}, u32[]{:S(2)}) collective-permute-start(bf16[96,3072]{1,0:T(8,128)(2,1)S(1)} %collective-permute-done.1.x_ref), channel_id=1, source_target_pairs={{0,32},{32,0},{64,96},{96,64},{1,33},{33,1},{65,97},{97,65},{2,34}... | collective-permute-start | bytes 1769480 | tf_op jit(solution)/shard_map/ppermute | solution.py:497
  26.4 1.4 %copy-start.4 = (bf16[32,18,16,128]{3,2,1,0:T(8,128)(2,1)}, bf16[32,18,16,128]{3,2,1,0:T(8,128)(2,1)S(1)}, u32[]{:S(2)}) copy-start(bf16[32,18,16,128]{3,2,1,0:T(8,128)(2,1)S(1)} %main.1) | copy-start | bytes 7077892
  27.8 10.9 %copy-start.11 = (s32[32,4]{0,1:T(4,128)S(1)}, s32[32,4]{0,1:T(4,128)}, u32[]{:S(2)}) copy-start(s32[32,4]{0,1:T(4,128)} %param.16) | copy-start | bytes 1540
  27.8 11.0 %copy-start.10 = (bf16[32,4,4]{0,2,1:T(4,128)(2,1)S(1)}, bf16[32,4,4]{0,2,1:T(4,128)(2,1)}, u32[]{:S(2)}) copy-start(bf16[32,4,4]{0,2,1:T(4,128)(2,1)} %param.17) | copy-start | bytes 3076
  27.8 45.5 %all-to-all-start = ((bf16[32,18,16,128]{3,2,1,0:T(8,128)(2,1)}), bf16[32,18,16,128]{3,2,1,0:T(8,128)(2,1)S(1)}, u32[]{:S(2)}, u32[]{:S(2)}) async-start(bf16[32,18,16,128]{3,2,1,0:T(8,128)(2,1)} %copy-done.4), calls=%async_computation | async-start | bytes 4718592 | tf_op jit(solution)/shard_map/all_to_all | solution.py:515

commit v6 on v4

--- a/solution.py
+++ b/solution.py
@@ -221,7 +221,7 @@
                     vl[jj, target, half * XQ : (half + 1) * XQ] = low
             return carry
 
-        lax.fori_loop(0, QUARTER // STRIP, strip, 0)
+        lax.fori_loop(0, QUARTER // STRIP, strip, 0, unroll=2)
 
 
 def near_kernel(focus_ref, slab_ref, xa_ref, xb_ref, fh, fl, left_ref, right_ref, fy_ref, fx_ref,
@@ -359,7 +359,7 @@
                         out[place, low_tile + tile] = joined.astype(jnp.bfloat16)
                 return carry
 
-            lax.fori_loop(0, devices // per_strip, strip, 0, unroll=4)
+            lax.fori_loop(0, devices // per_strip, strip, 0, unroll=8)
             low_row += devices * count
             low_tile += XP // per_tile
 

time: 84.9 us -> 84.3 us (level); the launches traced: 83.3 us -> 83.9 us
  no operation moved by 1% of the time
where the time goes in v6:
time: 84.3 us; the launch traced here: 83.9 us
  waiting for transfers between devices  35.6 us (42%)
  Pallas kernels  23.2 us (28%)
  starting transfers between devices  12.8 us (15%)
  local copies, waits for them, and re-layouts  9 us (11%)
  between operations  2.01 us (2%)
  other arithmetic  1.28 us (2%)
    all_to_all x1, waiting for transfers between devices, body(): lax.all_to_all(filtered, 'dev', split_axis=0, concat_axis=0, tiled=True)  34.4 us
    all_to_all x1, starting transfers between devices, body(): lax.all_to_all(filtered, 'dev', split_axis=0, concat_axis=0, tiled=True)  10.9 us
    pallas_call x1, Pallas kernels, run_project(): pl.pallas_call(project_kernel, in_specs=[scalar_spec()] * 2 + [vmem_spec(...  10.7 us
    unnamed x25, local copies, waits for them, and re-layouts  8.92 us
    pallas_call x1, Pallas kernels, run_main(): pl.pallas_call(main_kernel, in_specs=[vmem_spec()] * len(args), out_specs...  8.19 us
    pallas_call x1, Pallas kernels, run_near(): pl.pallas_call(near_kernel, in_specs=[scalar_spec()] * 2 + [vmem_spec()]...  2.92 us
    ppermute x3, starting transfers between devices, swap(): return lax.ppermute(block, 'slab', [(i, i ^ bit) for i in range(4)])  1.92 us
  transfers between devices with their start and end apart: 4, of which 3 were waited for; matrix products, arithmetic and copies ran while one was open for 2% of the time, Pallas kernels for 5%

profile of v6, /device:TPU:2, one launch (start us, length us, event | category | flops | bytes accessed | tf_op | source)
XLA Modules:
  0.0 83.9 jit_solution(13355023150912203367)
XLA Ops:
  0.0 0.0 collective-permute-start
  0.0 1.9 %collective-permute-start.1 = (bf16[96,3072]{1,0:T(8,128)(2,1)}, bf16[96,3072]{1,0:T(8,128)(2,1)S(1)}, u32[]{:S(2)}, u32[]{:S(2)}) collective-permute-start(bf16[96,3072]{1,0:T(8,128)(2,1)} %bitcast.8), channel_id=1, source_target_pairs={{0,64},{32,96},{64,0},{96,32},{1,65},{33,97},{65,1},{97,33},{2,66}... | collective-permute-start | bytes 1769480 | tf_op jit(solution)/shard_map/ppermute | solution.py:501
  3.2 1.3 %fusion = f32[]{:T(128)} fusion(f32[8]{0:T(128)} %param.14, s32[]{:T(128)} %bitcast.6), kind=kLoop, calls=%fused_computation.1 | loop fusion | flops 23 | bytes 40 | tf_op jit(solution)/shard_map/reduce_sum | solution.py:507
  5.1 0.0 collective-permute-done.xb_ref
  5.2 0.0 copy-start
  5.2 1.4 %copy-done = bf16[12,256,256]{2,1,0:T(8,128)(2,1)S(1)} copy-done((bf16[12,256,256]{2,1,0:T(8,128)(2,1)S(1)}, bf16[12,256,256]{2,1,0:T(8,128)(2,1)}, u32[]{:S(2)}) %copy-start) | copy-done | bytes 1572888
  6.6 1.4 %copy-done.2 = bf16[12,256,256]{2,1,0:T(8,128)(2,1)S(1)} copy-done((bf16[12,256,256]{2,1,0:T(8,128)(2,1)S(1)}, bf16[12,256,256]{2,1,0:T(8,128)(2,1)}, u32[]{:S(2)}) %copy-start.2) | copy-done | bytes 1572888
  8.0 1.1 %copy-done.5 = f32[2,2,192,192]{3,2,1,0:T(8,128)S(1)} copy-done((f32[2,2,192,192]{3,2,1,0:T(8,128)S(1)}, f32[2,2,192,192]{3,2,1,0:T(8,128)}, u32[]{:S(2)}) %copy-start.5) | copy-done | bytes 589848
  9.1 1.1 %copy-done.6 = bf16[1,96,3072]{2,1,0:T(8,128)(2,1)S(1)} copy-done((bf16[1,96,3072]{2,1,0:T(8,128)(2,1)S(1)}, bf16[1,96,3072]{2,1,0:T(8,128)(2,1)}, u32[]{:S(2)}) %copy-start.6) | copy-done | bytes 589848
  10.2 1.0 %copy-done.7 = f32[2,192,192]{2,1,0:T(8,128)S(1)} copy-done((f32[2,192,192]{2,1,0:T(8,128)S(1)}, f32[2,192,192]{2,1,0:T(8,128)}, u32[]{:S(2)}) %copy-start.7) | copy-done | bytes 294936
  11.2 0.7 copy-done.8
  11.9 0.7 copy-done.9
  12.6 2.9 %near.1 = (f32[12,192,256]{2,1,0:T(8,128)S(1)}, bf16[2,384,768]{2,1,0:T(8,128)(2,1)S(1)}, f32[12,2,256]{2,1,0:T(2,128)S(1)}) custom-call(f32[1]{0:T(128)S(6)} %add.7.focus_ref, s32[1]{0:T(128)} %bitcast.3.slab_ref, bf16[96,3072]{1,0:T(8,128)(2,1)S(1)} %bitcast.9, bf16[96,3072]{1,0:T(8,128)(2,1)S(1)} %collective-permute-done.xb_ref, ...), custom_call_target="tpu_custom_call" | custom-call | tf_op jit(solution)/shard_map/near/pallas_call | solution.py:272
  15.5 0.6 collective-permute-done.1.x_ref
  16.1 0.0 collective-permute-start.2
  16.1 1.4 %quarter.1 = f32[12,96,256]{2,1,0:T(8,128)S(1)} custom-call(bf16[96,3072]{1,0:T(8,128)(2,1)S(1)} %collective-permute-done.1.x_ref, bf16[12,256,256]{2,1,0:T(8,128)(2,1)S(1)} %copy-done.1, bf16[12,256,256]{2,1,0:T(8,128)(2,1)S(1)} %copy-done.3), custom_call_target="tpu_custom_call" | custom-call | tf_op jit(solution)/shard_map/quarter/pallas_call | solution.py:299
  17.5 0.6 collective-permute-done.2.xb
  18.1 8.2 %main.1 = bf16[32,18,16,128]{3,2,1,0:T(8,128)(2,1)S(1)} custom-call(bf16[96,3072]{1,0:T(8,128)(2,1)S(1)} %collective-permute-done.2.xb, f32[12,192,256]{2,1,0:T(8,128)S(1)} %get-tuple-element.15.near, f32[12,96,256]{2,1,0:T(8,128)S(1)} %quarter.1, bf16[2,384,768]{2,1,0:T(8,128)(2,1)S(1)} %get-tuple-element.17.mix, f32[12,2,256]{2,1,0:T(2,128)S(1)} %get-tuple-element.18.gain, ...), custom_call_target="tpu_custom_call" | custom-call | tf_op jit(solution)/shard_map/main/pallas_call | solution.py:372
  26.3 1.4 %copy-done.4 = bf16[32,18,16,128]{3,2,1,0:T(8,128)(2,1)} copy-done((bf16[32,18,16,128]{3,2,1,0:T(8,128)(2,1)}, bf16[32,18,16,128]{3,2,1,0:T(8,128)(2,1)S(1)}, u32[]{:S(2)}) %copy-start.4) | copy-done | bytes 2359320
  27.8 10.9 %all-to-all-start = ((bf16[32,18,16,128]{3,2,1,0:T(8,128)(2,1)}), bf16[32,18,16,128]{3,2,1,0:T(8,128)(2,1)S(1)}, u32[]{:S(2)}, u32[]{:S(2)}) async-start(bf16[32,18,16,128]{3,2,1,0:T(8,128)(2,1)} %copy-done.4), calls=%async_computation | async-start | bytes 4718592 | tf_op jit(solution)/shard_map/all_to_all | solution.py:518
  38.7 0.1 copy.15.off_ref
  38.8 0.1 copy.16.weight_ref
  38.8 34.4 %all-to-all-done.x = bf16[32,18,16,128]{3,2,1,0:T(8,128)(2,1)S(1)} async-done(((bf16[32,18,16,128]{3,2,1,0:T(8,128)(2,1)}), bf16[32,18,16,128]{3,2,1,0:T(8,128)(2,1)S(1)}, u32[]{:S(2)}, u32[]{:S(2)}) %all-to-all-start) | async-done | bytes 2359328 | tf_op jit(solution)/shard_map/all_to_all | solution.py:518
  73.2 10.7 %project.1 = f32[12,4,3072]{2,1,0:T(4,128)} custom-call(s32[32,4]{1,0:T(8,128)S(1)} %copy.15.off_ref, f32[32,16]{1,0:T(8,128)S(1)} %copy.16.weight_ref, bf16[32,18,16,128]{3,2,1,0:T(8,128)(2,1)S(1)} %all-to-all-done.x), custom_call_target="tpu_custom_call" | custom-call | tf_op jit(solution)/shard_map/project/pallas_call | solution.py:484
  (15 shorter events, 0.0 us)
Async XLA Ops:
  0.0 5.1 %collective-permute-start = (bf16[96,3072]{1,0:T(8,128)(2,1)}, bf16[96,3072]{1,0:T(8,128)(2,1)S(1)}, u32[]{:S(2)}, u32[]{:S(2)}) collective-permute-start(bf16[96,3072]{1,0:T(8,128)(2,1)} %bitcast.7), channel_id=1, source_target_pairs={{0,32},{32,0},{64,96},{96,64},{1,33},{33,1},{65,97},{97,65},{2,34}... | collective-permute-start | bytes 1769480 | tf_op jit(solution)/shard_map/ppermute | solution.py:501
  0.0 16.1 %collective-permute-start.1 = (bf16[96,3072]{1,0:T(8,128)(2,1)}, bf16[96,3072]{1,0:T(8,128)(2,1)S(1)}, u32[]{:S(2)}, u32[]{:S(2)}) collective-permute-start(bf16[96,3072]{1,0:T(8,128)(2,1)} %bitcast.8), channel_id=1, source_target_pairs={{0,64},{32,96},{64,0},{96,32},{1,65},{33,97},{65,1},{97,33},{2,66}... | collective-permute-start | bytes 1769480 | tf_op jit(solution)/shard_map/ppermute | solution.py:501
  5.2 1.4 %copy-start = (bf16[12,256,256]{2,1,0:T(8,128)(2,1)S(1)}, bf16[12,256,256]{2,1,0:T(8,128)(2,1)}, u32[]{:S(2)}) copy-start(bf16[12,256,256]{2,1,0:T(8,128)(2,1)} %constant.20.clone.fh) | copy-start | bytes 4718596
  6.6 1.4 %copy-start.2 = (bf16[12,256,256]{2,1,0:T(8,128)(2,1)S(1)}, bf16[12,256,256]{2,1,0:T(8,128)(2,1)}, u32[]{:S(2)}) copy-start(bf16[12,256,256]{2,1,0:T(8,128)(2,1)} %constant.21.clone.fl) | copy-start | bytes 4718596
  8.0 1.1 %copy-start.5 = (f32[2,2,192,192]{3,2,1,0:T(8,128)S(1)}, f32[2,2,192,192]{3,2,1,0:T(8,128)}, u32[]{:S(2)}) copy-start(f32[2,2,192,192]{3,2,1,0:T(8,128)} %constant.23.clone.right_ref) | copy-start | bytes 1769476
  9.1 1.1 %copy-start.6 = (bf16[1,96,3072]{2,1,0:T(8,128)(2,1)S(1)}, bf16[1,96,3072]{2,1,0:T(8,128)(2,1)}, u32[]{:S(2)}) copy-start(bf16[1,96,3072]{2,1,0:T(8,128)(2,1)} %param.12) | copy-start | bytes 1769476
  10.2 1.0 %copy-start.7 = (f32[2,192,192]{2,1,0:T(8,128)S(1)}, f32[2,192,192]{2,1,0:T(8,128)}, u32[]{:S(2)}) copy-start(f32[2,192,192]{2,1,0:T(8,128)} %constant.22.clone.left_ref) | copy-start | bytes 884740
  11.2 0.7 copy-start.8
  11.9 0.7 copy-start.9
  12.6 3.6 %copy-start.1 = (bf16[12,256,256]{2,1,0:T(8,128)(2,1)S(1)}, bf16[12,256,256]{2,1,0:T(8,128)(2,1)}, u32[]{:S(2)}) copy-start(bf16[12,256,256]{2,1,0:T(8,128)(2,1)} %constant.20.clone.fh) | copy-start | bytes 4718596
  12.6 3.6 %copy-start.3 = (bf16[12,256,256]{2,1,0:T(8,128)(2,1)S(1)}, bf16[12,256,256]{2,1,0:T(8,128)(2,1)}, u32[]{:S(2)}) copy-start(bf16[12,256,256]{2,1,0:T(8,128)(2,1)} %constant.21.clone.fl) | copy-start | bytes 4718596
  16.1 2.0 %collective-permute-start.2 = (bf16[96,3072]{1,0:T(8,128)(2,1)S(1)}, bf16[96,3072]{1,0:T(8,128)(2,1)S(1)}, u32[]{:S(2)}, u32[]{:S(2)}) collective-permute-start(bf16[96,3072]{1,0:T(8,128)(2,1)S(1)} %collective-permute-done.1.x_ref), channel_id=1, source_target_pairs={{0,32},{32,0},{64,96},{96,64},{1,33},{33,1},{65,97},{97,65},{2,34}... | collective-permute-start | bytes 1769480 | tf_op jit(solution)/shard_map/ppermute | solution.py:501
  26.3 1.4 %copy-start.4 = (bf16[32,18,16,128]{3,2,1,0:T(8,128)(2,1)}, bf16[32,18,16,128]{3,2,1,0:T(8,128)(2,1)S(1)}, u32[]{:S(2)}) copy-start(bf16[32,18,16,128]{3,2,1,0:T(8,128)(2,1)S(1)} %main.1) | copy-start | bytes 7077892
  27.8 10.9 %copy-start.11 = (s32[32,4]{0,1:T(4,128)S(1)}, s32[32,4]{0,1:T(4,128)}, u32[]{:S(2)}) copy-start(s32[32,4]{0,1:T(4,128)} %param.16) | copy-start | bytes 1540
  27.8 11.0 %copy-start.10 = (bf16[32,4,4]{0,2,1:T(4,128)(2,1)S(1)}, bf16[32,4,4]{0,2,1:T(4,128)(2,1)}, u32[]{:S(2)}) copy-start(bf16[32,4,4]{0,2,1:T(4,128)(2,1)} %param.17) | copy-start | bytes 3076
  27.8 45.5 %all-to-all-start = ((bf16[32,18,16,128]{3,2,1,0:T(8,128)(2,1)}), bf16[32,18,16,128]{3,2,1,0:T(8,128)(2,1)S(1)}, u32[]{:S(2)}, u32[]{:S(2)}) async-start(bf16[32,18,16,128]{3,2,1,0:T(8,128)(2,1)} %copy-done.4), calls=%async_computation | async-start | bytes 4718592 | tf_op jit(solution)/shard_map/all_to_all | solution.py:518
